TPU v7x, 32 devices: a whole 2x2x4 slice. The times are simulated.
32 devices in a mesh: fsdp: 8 (over z, y), seq: 4 (over x, core).
Axes of the slice: x: 2, y: 2, z: 4, core: 2. Of those that a mesh axis runs over, the one named last changes fastest.
Arguments:
- queries: bfloat16 [4096, 4096], P(('fsdp', 'seq')), may hold values from -6 to 6
- keys: bfloat16 [4096, 4096], P(('fsdp', 'seq')), may hold values from -6 to 6
- values: bfloat16 [4096, 4096], P(('fsdp', 'seq')), may hold values from -6 to 6
- cotangent: bfloat16 [4096, 4096], P(('fsdp', 'seq')), may hold values from -8 to 8
- out_weight: bfloat16 [4096, 4096], P('seq', 'fsdp'), may hold values from -0.09375 to 0.09375
- short_taps: float32 [3, 7, 4096], P(None, None, 'seq'), may hold values from -2 to 2
- long_taps: float32 [128, 256], P(None, 'seq'), may hold values from -0.5 to 0.5
- skip_gain: float32 [4096], P('seq'), may hold values from -1 to 1
Outputs:
- query_grad: bfloat16 [4096, 4096], P(('fsdp', 'seq'))
- key_grad: bfloat16 [4096, 4096], P(('fsdp', 'seq'))
- value_grad: bfloat16 [4096, 4096], P(('fsdp', 'seq'))
- weight_grad: float32 [4096, 4096], P('seq', 'fsdp')
- short_grad: float32 [3, 7, 4096], P(None, None, 'seq')
- long_grad: float32 [128, 256], P(None, 'seq')
- gain_grad: float32 [4096], P('seq')
All inputs are finite; a program needn't handle non-finite values.
Results may differ from a plain program's by a relative error of at most 0.0075.
Values may be sent and summed in bfloat16 or wider, within the bound.
No kernel may reach another device: no remote copies, remote signals or barrier semaphores. Data moves between devices by JAX's collectives and lax.ppermute only.
A program may use at most 256 MiB of HBM per device.

v0:
```python
import functools

import jax
import jax.numpy as jnp
from jax import lax
from jax.experimental import pallas as pl
from jax.experimental.pallas import tpu as pltpu
from jax.sharding import Mesh
from jax.sharding import PartitionSpec as P

SHORT = 7
LTAPS = 128
LANES = 128
PAD = 16
Z = 4
F32 = jnp.float32
BF16 = jnp.bfloat16


def params():
    return pltpu.CompilerParams(vmem_limit_bytes=60 * 2**20)


def tables_kernel(fwd_ref, bwd_ref, tf_ref, tb_ref):
    for g in range(fwd_ref.shape[0]):
        rows = slice(g * LTAPS, (g + 1) * LTAPS)
        for src, dst in ((fwd_ref, tf_ref), (bwd_ref, tb_ref)):
            wide = jnp.broadcast_to(src[g : g + 1, :], (LTAPS, 2 * LTAPS))
            dst[rows, :] = pltpu.roll(wide, 0, 1, stride=1, stride_axis=0).astype(BF16)


def make_tables(long_taps):
    by_group = long_taps.T
    groups = by_group.shape[0]
    fwd = jnp.pad(by_group[:, ::-1], ((0, 0), (1, LTAPS - 1)))
    bwd = jnp.pad(by_group, ((0, 0), (0, LTAPS)))
    per = 8
    row_spec = pl.BlockSpec((per, 2 * LTAPS), lambda i: (i, 0))
    tab_spec = pl.BlockSpec((per * LTAPS, 2 * LTAPS), lambda i: (i, 0))
    shape = jax.ShapeDtypeStruct((groups * LTAPS, 2 * LTAPS), BF16)
    return pl.pallas_call(
        tables_kernel,
        grid=(groups // per,),
        in_specs=[row_spec, row_spec],
        out_specs=[tab_spec, tab_spec],
        out_shape=[shape, shape],
        compiler_params=params(),
        name="tables",
    )(fwd, bwd)


def pick_groups(wide, col, rows, per):
    lane_group = lax.broadcasted_iota(jnp.int32, (rows, LANES), 1) // (LANES // per)
    cols = slice(col * LANES, (col + 1) * LANES)
    out = wide[0:rows, cols]
    for g in range(1, per):
        out = jnp.where(lane_group == g, wide[g * rows : (g + 1) * rows, cols], out)
    return out


def features_of(taps_ref, row, xf, i, begin):
    total = taps_ref[row, 0:1] * xf[i, PAD + begin : PAD + begin + LTAPS]
    for j in range(1, SHORT):
        total = total + taps_ref[row, j : j + 1] * xf[i, PAD + begin - j : PAD + begin - j + LTAPS]
    return total


def forward_kernel(
    place_ref, x_ref, h_ref, taps_ref, skip_ref, tab_ref, _, mixed_ref, f_ref, filt_ref, xf, pf, pb, wide
):
    blocks, _, rows, _ = x_ref.shape
    tokens = blocks * rows
    per = tab_ref.shape[0] // LTAPS
    for i in range(3):
        xf[i, 0:PAD] = h_ref[i * PAD : (i + 1) * PAD].astype(F32)
        for b in range(blocks):
            begin = PAD + b * rows
            xf[i, begin : begin + rows] = x_ref[b, i].astype(F32)
    pb[0:LTAPS] = h_ref[3 * PAD : 3 * PAD + LTAPS]
    for begin in range(0, tokens, LTAPS):
        own = slice(begin, begin + LTAPS)
        f1 = features_of(taps_ref, 1, xf, 1, begin)
        f2 = features_of(taps_ref, 2, xf, 2, begin)
        prod = f1 * f2
        f_ref[1, own] = f1
        f_ref[2, own] = f2
        f_ref[0, own] = features_of(taps_ref, 0, xf, 0, begin)
        pf[own] = prod
        pb[LTAPS + begin : 2 * LTAPS + begin] = prod.astype(BF16)
    skip = skip_ref[...]
    for b in range(0, tokens // LTAPS, 2):
        low = b * LTAPS
        windows = jnp.concatenate([pb[low : low + 2 * LTAPS], pb[low + LTAPS : low + 3 * LTAPS]], axis=1)
        wide[...] = jnp.dot(tab_ref[...], windows, preferred_element_type=F32)
        for n in range(2):
            own = slice(low + n * LTAPS, low + (n + 1) * LTAPS)
            filtered = pick_groups(wide, n, LTAPS, per) + skip * pf[own]
            filt_ref[own] = filtered
            mixed = f_ref[0, own] * filtered
            there = pl.multiple_of(place_ref[b + n] * LTAPS, LTAPS)
            mixed_ref[:, pl.ds(there, LTAPS)] = mixed.T.astype(BF16)


def forward(x, halo, short_taps, skip, table, place, chunk, chunks, after):
    blocks, _, rows, cols = x.shape
    cols //= chunks
    tokens = blocks * rows
    tiles = cols // LANES
    first = chunk * tiles
    tab_rows = table.shape[0] * LANES // skip.shape[1]
    return pl.pallas_call(
        forward_kernel,
        grid_spec=pltpu.PrefetchScalarGridSpec(
            num_scalar_prefetch=1,
            grid=(tiles,),
            in_specs=[
                pl.BlockSpec((blocks, 3, rows, LANES), lambda c, _: (0, 0, 0, first + c)),
                pl.BlockSpec((halo.shape[0], LANES), lambda c, _: (0, first + c)),
                pl.BlockSpec((3, SHORT, LANES), lambda c, _: (0, 0, first + c)),
                pl.BlockSpec((1, LANES), lambda c, _: (0, first + c)),
                pl.BlockSpec((tab_rows, 2 * LTAPS), lambda c, _: (first + c, 0)),
                pl.BlockSpec(memory_space=pl.ANY),
            ],
            out_specs=[
                pl.BlockSpec((LANES, tokens), lambda c, _: (c, 0)),
                pl.BlockSpec((3, tokens, LANES), lambda c, _: (0, 0, c)),
                pl.BlockSpec((tokens, LANES), lambda c, _: (0, c)),
            ],
            scratch_shapes=[
                pltpu.VMEM((3, PAD + tokens, LANES), F32),
                pltpu.VMEM((tokens, LANES), F32),
                pltpu.VMEM((LTAPS + tokens, LANES), BF16),
                pltpu.VMEM((tab_rows, 2 * LTAPS), F32),
            ],
        ),
        out_shape=[
            jax.ShapeDtypeStruct((cols, tokens), BF16),
            jax.ShapeDtypeStruct((3, tokens, cols), F32),
            jax.ShapeDtypeStruct((tokens, cols), F32),
        ],
        compiler_params=params(),
        name="forward",
    )(place, x, halo, short_taps, skip, table, after)


def sum_by_lag(gram):
    wide = gram.shape[1]
    parts = [gram[i : i + 8] for i in range(0, gram.shape[0], 8)]
    step = 8
    while len(parts) > 1:
        parts = [
            parts[k] + pltpu.roll(parts[k + 1], wide - step, 1) for k in range(0, len(parts), 2)
        ]
        step *= 2
    total = parts[0]
    row = lax.broadcasted_iota(jnp.int32, total.shape, 0)
    for bit in (1, 2, 4):
        total = jnp.where((row & bit) != 0, pltpu.roll(total, wide - bit, 1), total)
    return jnp.sum(total[:, :LTAPS], axis=0, keepdims=True)


def backward_kernel(
    mo_ref, mr_ref, f_ref, filt_ref, x_ref, n_ref, taps_ref, skip_ref, tab_ref,
    grad_ref, short_ref, long_ref, db, fg, wide, left, right,
):
    blocks, _, rows, _ = x_ref.shape
    tokens = blocks * rows
    per = tab_ref.shape[0] // LTAPS
    count = tokens // LTAPS
    skip = skip_ref[...]
    lane_group = lax.broadcasted_iota(jnp.int32, (1, LANES), 1) // (LANES // per)
    gain = jnp.zeros((8, LANES), F32)
    for b in range(count):
        own = slice(b * LTAPS, (b + 1) * LTAPS)
        mixed_grad = mo_ref[own] + mr_ref[own].astype(F32)
        slope = mixed_grad * f_ref[0, own]
        db[own] = slope.astype(BF16)
        fg[0, own] = mixed_grad * filt_ref[own]
        fg[1, own] = skip * slope
        prod = f_ref[1, own] * f_ref[2, own]
        gain = gain + jnp.sum((prod * slope).reshape(LTAPS // 8, 8, LANES), axis=0)
        prod_b = prod.astype(BF16)
        for g in range(per):
            keep = (lane_group == g).astype(F32).astype(BF16)
            left[g * LTAPS : (g + 1) * LTAPS, b * LANES : (b + 1) * LANES] = prod_b * keep
    db[tokens : tokens + LTAPS + PAD] = n_ref[0 : LTAPS + PAD]
    db[tokens + LTAPS + PAD :] = jnp.zeros((LTAPS - PAD, LANES), BF16)
    for b in range(count):
        right[:, b * LANES : (b + 1) * LANES] = db[b * LTAPS : (b + 2) * LTAPS]
    for b in range(0, count, 2):
        wide[...] = jnp.dot(
            tab_ref[...], right[:, b * LANES : (b + 2) * LANES], preferred_element_type=F32
        )
        for n in range(2):
            own = slice((b + n) * LTAPS, (b + n + 1) * LTAPS)
            grad = pick_groups(wide, n, LTAPS, per) + fg[1, own]
            fg[1, own] = grad * f_ref[2, own]
            fg[2, own] = grad * f_ref[1, own]
    few = jnp.concatenate([tab_ref[g * LTAPS : g * LTAPS + PAD] for g in range(per)], axis=0)
    edge = jnp.dot(few, db[tokens : tokens + 2 * LTAPS], preferred_element_type=F32)
    begin = LTAPS + PAD
    grad = pick_groups(edge, 0, PAD, per) + skip * n_ref[0:PAD].astype(F32)
    fg[1, tokens : tokens + PAD] = grad * n_ref[begin + PAD : begin + 2 * PAD].astype(F32)
    fg[2, tokens : tokens + PAD] = grad * n_ref[begin : begin + PAD].astype(F32)
    fg[0, tokens : tokens + PAD] = n_ref[begin + 2 * PAD : begin + 3 * PAD].astype(F32)
    for i in range(3):
        sums = [jnp.zeros((8, LANES), F32) for _ in range(SHORT)]
        for b in range(count):
            low = b * LTAPS
            inputs = x_ref[b, i].astype(F32)
            total = None
            for j in range(SHORT):
                later = fg[i, low + j : low + j + LTAPS]
                term = taps_ref[i, j : j + 1] * later
                total = term if total is None else total + term
                sums[j] = sums[j] + jnp.sum((later * inputs).reshape(LTAPS // 8, 8, LANES), axis=0)
            grad_ref[b, i] = total.astype(BF16)
        for j in range(SHORT):
            short_ref[i, j : j + 1] = jnp.sum(sums[j], axis=0, keepdims=True)
        short_ref[i, SHORT : SHORT + 1] = jnp.sum(gain, axis=0, keepdims=True)
    wide[...] = lax.dot_general(left[...], right[...], (((1,), (1,)), ((), ())), preferred_element_type=F32)
    for g in range(per):
        gram = wide[g * LTAPS : (g + 1) * LTAPS]
        long_ref[g : g + 1] = sum_by_lag(gram)


def backward(mixed_own, mixed_rest, feats, filt, x, later, short_taps, skip, table, chunk, chunks):
    blocks, _, rows, cols = x.shape
    cols //= chunks
    tokens = blocks * rows
    tiles = cols // LANES
    first = chunk * tiles
    tab_rows = table.shape[0] * LANES // skip.shape[1]
    per = tab_rows // LTAPS
    tok = pl.BlockSpec((tokens, LANES), lambda c: (0, first + c))
    return pl.pallas_call(
        backward_kernel,
        grid=(tiles,),
        in_specs=[
            tok,
            tok,
            pl.BlockSpec((3, tokens, LANES), lambda c: (0, 0, c)),
            pl.BlockSpec((tokens, LANES), lambda c: (0, c)),
            pl.BlockSpec((blocks, 3, rows, LANES), lambda c: (0, 0, 0, first + c)),
            pl.BlockSpec((later.shape[0], LANES), lambda c: (0, first + c)),
            pl.BlockSpec((3, SHORT, LANES), lambda c: (0, 0, first + c)),
            pl.BlockSpec((1, LANES), lambda c: (0, first + c)),
            pl.BlockSpec((tab_rows, 2 * LTAPS), lambda c: (first + c, 0)),
        ],
        out_specs=[
            pl.BlockSpec((blocks, 3, rows, LANES), lambda c: (0, 0, 0, c)),
            pl.BlockSpec((3, SHORT + 1, LANES), lambda c: (0, 0, c)),
            pl.BlockSpec((per, LTAPS), lambda c: (c, 0)),
        ],
        out_shape=[
            jax.ShapeDtypeStruct((blocks, 3, rows, cols), BF16),
            jax.ShapeDtypeStruct((3, SHORT + 1, cols), F32),
            jax.ShapeDtypeStruct((tiles * per, LTAPS), F32),
        ],
        scratch_shapes=[
            pltpu.VMEM((tokens + 2 * LTAPS, LANES), BF16),
            pltpu.VMEM((3, tokens + PAD, LANES), F32),
            pltpu.VMEM((tab_rows, 2 * LTAPS), F32),
            pltpu.VMEM((tab_rows, tokens), BF16),
            pltpu.VMEM((2 * LTAPS, tokens), BF16),
        ],
        compiler_params=params(),
        cost_estimate=pl.CostEstimate(flops=10**11, bytes_accessed=36 * tokens * cols, transcendentals=0),
        name="backward",
    )(mixed_own, mixed_rest, feats, filt, x, later, short_taps, skip, table)


def pack_kernel(*refs):
    out_ref = refs[-1]
    for i, ref in enumerate(refs[:3]):
        out_ref[0, i] = ref[...]


def pack(arrays, seq):
    rows, width = arrays[0].shape
    cols = width // seq
    return pl.pallas_call(
        pack_kernel,
        grid=(seq,),
        in_specs=[pl.BlockSpec((rows, cols), lambda s: (0, s))] * 3,
        out_specs=pl.BlockSpec((1, 3, rows, cols), lambda s: (s, 0, 0, 0)),
        out_shape=jax.ShapeDtypeStruct((seq, 3, rows, cols), BF16),
        compiler_params=params(),
        name="pack",
    )(*arrays)


def unpack_kernel(*refs):
    parts, outs = refs[:-3], refs[-3:]
    cols = parts[0].shape[3]
    for n, part in enumerate(parts):
        for i, out in enumerate(outs):
            out[:, n * cols : (n + 1) * cols] = part[0, i]


def unpack(parts):
    seq, _, rows, cols = parts[0].shape
    wide = cols * len(parts)
    shape = jax.ShapeDtypeStruct((rows, seq * wide), BF16)
    return pl.pallas_call(
        unpack_kernel,
        grid=(seq,),
        in_specs=[pl.BlockSpec((1, 3, rows, cols), lambda s: (s, 0, 0, 0))] * len(parts),
        out_specs=[pl.BlockSpec((rows, wide), lambda s: (0, s))] * 3,
        out_shape=[shape] * 3,
        compiler_params=params(),
        name="unpack",
    )(*parts)


def along(block, axis, distance):
    size = lax.axis_size(axis)
    return lax.ppermute(block, axis, [(i, i + distance) for i in range(size) if 0 <= i + distance < size])


def around(block, axis, distance):
    size = lax.axis_size(axis)
    return lax.ppermute(block, axis, [(i, (i + distance) % size) for i in range(size)])


def across(block, axis, bit):
    return lax.ppermute(block, axis, [(i, i ^ bit) for i in range(lax.axis_size(axis))])


def bits_of(axis):
    size = lax.axis_size(axis)
    return [1 << n for n in range(size.bit_length() - 1)]


def sum_over(value, axes):
    for axis in axes:
        for bit in bits_of(axis):
            value = value + across(value, axis, bit)
    return value


def split_kernel(y_ref, *refs):
    count = (len(refs) - 1) // 2
    for n in range(count):
        refs[count + 1 + n][...] = refs[n][...]


def split_cotangent(cotangent, y, ys, col_part, after):
    rows, width = cotangent.shape

    def source(step):
        return pl.BlockSpec((rows, col_part), lambda z, y_ref: (0, z * ys + (y_ref[0] + step) % ys))

    return pl.pallas_call(
        split_kernel,
        grid_spec=pltpu.PrefetchScalarGridSpec(
            num_scalar_prefetch=1,
            grid=(Z,),
            in_specs=[source(step) for step in range(ys)] + [pl.BlockSpec(memory_space=pl.ANY)],
            out_specs=[pl.BlockSpec((rows, col_part), lambda z, _: (0, z))] * ys,
        ),
        out_shape=[jax.ShapeDtypeStruct((rows, width // ys), BF16)] * ys,
        compiler_params=params(),
        name="split",
    )(y.reshape(1), *([cotangent] * ys), after)


def join_kernel(axis, count, *refs):
    out = refs[-1]
    for n in range(count):
        size = refs[n].shape[axis]
        here = slice(n * size, (n + 1) * size)
        if axis == 0:
            out[here] = refs[n][...]
        else:
            out[:, here] = refs[n][...]


def join(parts, axis, after=()):
    shape = list(parts[0].shape)
    tile = shape[-1] // Z
    block = pl.BlockSpec((*shape[:-1], tile), lambda i: (0, 0, 0, i))
    shape[axis] *= len(parts)
    return pl.pallas_call(
        functools.partial(join_kernel, axis, len(parts)),
        grid=(Z,),
        in_specs=[block] * len(parts) + [pl.BlockSpec(memory_space=pl.ANY)] * len(after),
        out_specs=pl.BlockSpec((*shape[:-1], tile), lambda i: (0, 0, 0, i)),
        out_shape=jax.ShapeDtypeStruct(tuple(shape), BF16),
        compiler_params=params(),
        name="join",
    )(*parts, *after)


def own_cotangent(cotangent, col_part, after):
    ys, y = lax.axis_size("y"), lax.axis_index("y")
    held = split_cotangent(cotangent, y, ys, col_part, after)
    held = [around(part, "y", step) if step else part for step, part in enumerate(held)]
    return join([part[None, None] for part in held], 0)


def gather_cotangent(held, after):
    bits = bits_of("seq")
    for bit in reversed(bits[1:]):
        held = join([held, across(held, "seq", bit)], 1, after)
    return held, across(held, "seq", bits[0])


def mixed_grad_kernel(waits, place_ref, a_ref, b_ref, w_ref, *refs):
    out_ref, head_ref = refs[waits : waits + 2]
    found = refs[-1]
    _, count, rows, _ = a_ref.shape
    tokens = count * rows
    pieces = jnp.concatenate([ref[...].reshape(tokens, -1) for ref in (a_ref, b_ref)], axis=0)
    found[...] = contract(pieces, w_ref[...], 1)
    for block in range(2 * count):
        there = pl.multiple_of(place_ref[block] * rows, rows)
        out_ref[block * rows : (block + 1) * rows] = found[pl.ds(there, rows)].astype(out_ref.dtype)
    head_ref[...] = out_ref[0 : LTAPS + PAD]


def mixed_grad(cots, weights, place, step, dtype, after, passed=False):
    _, count, rows, width = cots[0].shape
    tokens = 2 * count * rows
    cols = weights.shape[0]
    tile = min(cols, 2 * LANES)
    piece = pl.BlockSpec((1, count, rows, width), lambda i, _: (step, 0, 0, 0))
    return pl.pallas_call(
        functools.partial(mixed_grad_kernel, len(after)),
        grid_spec=pltpu.PrefetchScalarGridSpec(
            num_scalar_prefetch=1,
            grid=(cols // tile,),
            in_specs=[
                piece,
                piece,
                pl.BlockSpec((tile, width), lambda i, _: (i, 0)),
            ]
            + [pl.BlockSpec(memory_space=pl.ANY)] * len(after),
            out_specs=[
                pl.BlockSpec((tokens, tile), lambda i, _: (0, i)),
                pl.BlockSpec((LTAPS + PAD, tile), lambda i, _: (0, i)),
            ]
            + [pl.BlockSpec(memory_space=pl.ANY)] * passed,
            scratch_shapes=[pltpu.VMEM((tokens, tile), F32)],
        ),
        input_output_aliases={4: 2} if passed else {},
        out_shape=[
            jax.ShapeDtypeStruct((tokens, cols), dtype),
            jax.ShapeDtypeStruct((LTAPS + PAD, cols), dtype),
        ]
        + [jax.ShapeDtypeStruct(after[0].shape, after[0].dtype)] * passed,
        compiler_params=params(),
        name="mixed_grad",
    )(place, *cots, weights, *after)


def weight_grad_kernel(scale, a_ref, b_ref, *refs):
    steps, count, rows, tile = a_ref.shape
    tokens = count * rows
    mixed, out = refs[:steps], refs[-1]
    total = None
    for step in range(steps):
        for n, ref in enumerate((a_ref, b_ref)):
            left = mixed[step][:, n * tokens : (n + 1) * tokens]
            term = jnp.dot(left, ref[step].reshape(tokens, tile), preferred_element_type=F32)
            total = term if total is None else total + term
    out[...] = (total * scale).astype(BF16)


def weight_grad(cots, mixed, chunk, chunks, scale, target, after):
    steps, count, rows, width = cots[0].shape
    part, tokens = mixed[0].shape
    tile = width // Z
    piece = pl.BlockSpec((steps, count, rows, tile), lambda i: (0, 0, 0, i))
    extra = [*after] + ([] if target is None else [target])
    return pl.pallas_call(
        functools.partial(weight_grad_kernel, scale),
        grid=(Z,),
        in_specs=[piece, piece]
        + [pl.BlockSpec((part, tokens), lambda i: (0, 0))] * len(mixed)
        + [pl.BlockSpec(memory_space=pl.ANY)] * len(extra),
        out_specs=pl.BlockSpec((part, tile), lambda i: (chunk, i)),
        out_shape=jax.ShapeDtypeStruct((part * chunks, width), BF16),
        input_output_aliases={} if target is None else {2 + len(mixed) + len(after): 0},
        compiler_params=params(),
        name="weight_grad",
    )(*cots, *mixed, *extra)


def tail_kernel(x_ref, before_ref, taps_ref, *refs):
    out_ref, xf = refs[-2:]
    rows = x_ref.shape[2]
    for i in range(3):
        out_ref[i * PAD : (i + 1) * PAD] = x_ref[0, i, rows - PAD :]
    for tile in range(x_ref.shape[3] // LANES):
        cols = slice(tile * LANES, (tile + 1) * LANES)
        taps = taps_ref[:, :, cols]
        prod = None
        for i in (1, 2):
            xf[tile, i - 1, 0:PAD] = before_ref[0, i, :, cols].astype(F32)
            xf[tile, i - 1, PAD:] = x_ref[0, i, :, cols].astype(F32)
            feature = taps[i, 0:1] * xf[tile, i - 1, PAD : PAD + rows]
            for j in range(1, SHORT):
                feature = feature + taps[i, j : j + 1] * xf[tile, i - 1, PAD - j : PAD - j + rows]
            prod = feature if prod is None else prod * feature
        out_ref[3 * PAD :, cols] = prod.astype(BF16)


def tail_of(x, short_taps, after):
    seq, _, rows, cols = x.shape
    wide = min(cols, 4 * LANES)
    out_rows = 3 * PAD + rows
    return pl.pallas_call(
        tail_kernel,
        grid=(cols // wide,),
        in_specs=[
            pl.BlockSpec((1, 3, rows, wide), lambda c: (seq - 1, 0, 0, c)),
            pl.BlockSpec((1, 3, PAD, wide), lambda c: (seq - 2, 0, rows // PAD - 1, c)),
            pl.BlockSpec((3, SHORT, wide), lambda c: (0, 0, c)),
        ]
        + [pl.BlockSpec(memory_space=pl.ANY)] * len(after),
        out_specs=pl.BlockSpec((out_rows, wide), lambda c: (0, c)),
        out_shape=jax.ShapeDtypeStruct((out_rows, cols), BF16),
        scratch_shapes=[pltpu.VMEM((wide // LANES, 2, PAD + rows, LANES), F32)],
        compiler_params=params(),
        name="tail",
    )(x, x, short_taps, *after)


def head_kernel(chunks, mo_ref, mr_ref, *refs):
    out_ref = refs[-1]
    edge = LTAPS + PAD
    part = out_ref.shape[1] // chunks
    for h in range(chunks):
        own = slice(h * part, (h + 1) * part)
        f_ref, filt_ref = refs[2 * h : 2 * h + 2]
        mixed = mo_ref[:, own] + mr_ref[:, own].astype(F32)
        out_ref[0:edge, own] = (mixed * f_ref[0]).astype(BF16)
        out_ref[edge : edge + PAD, own] = f_ref[1, 0:PAD].astype(BF16)
        out_ref[edge + PAD : edge + 2 * PAD, own] = f_ref[2, 0:PAD].astype(BF16)
        out_ref[edge + 2 * PAD :, own] = (mixed[0:PAD] * filt_ref[0:PAD]).astype(BF16)


def head_of(mixed_own, mixed_rest, mixers, after):
    edge, cols = LTAPS + PAD, mixed_own.shape[1]
    part = cols // len(mixers)
    whole = pl.BlockSpec((edge, cols), lambda i: (0, 0))
    feat_specs = [
        pl.BlockSpec((3, edge, part), lambda i: (0, 0, 0)),
        pl.BlockSpec((edge, part), lambda i: (0, 0)),
    ]
    return pl.pallas_call(
        functools.partial(head_kernel, len(mixers)),
        grid=(1,),
        in_specs=[whole, whole] + feat_specs * len(mixers) + [pl.BlockSpec(memory_space=pl.ANY)] * len(after),
        out_specs=pl.BlockSpec((edge + 3 * PAD, cols), lambda i: (0, 0)),
        out_shape=jax.ShapeDtypeStruct((edge + 3 * PAD, cols), BF16),
        compiler_params=params(),
        name="head",
    )(mixed_own, mixed_rest, *[array for mixer in mixers for array in mixer[1:]], *after)


def contract(a, b, dim):
    return lax.dot_general(a, b, (((dim,), (dim,)), ((), ())), preferred_element_type=F32)


def places(seq):
    bits = bits_of("seq")
    source = lax.iota(jnp.int32, seq) ^ lax.axis_index("seq")
    return sum(((source >> n) & 1) << (len(bits) - 1 - n) for n in range(len(bits)))


def body(queries, keys, values, cotangent, out_weight, short_taps, long_taps, skip_gain):
    rows, width = queries.shape
    col_part = out_weight.shape[1]
    seq, ys = lax.axis_size("seq"), lax.axis_size("y")
    cols = width // seq
    chunks = 2 if cols % (2 * LANES) == 0 else 1
    groups = long_taps.shape[1]
    fsdp = ("z", "y")
    grad_scale = float(rows * seq * ys * Z) ** (-0.5)

    weights = lax.all_gather(out_weight, "z", axis=1, tiled=True)
    fwd_table, bwd_table = make_tables(long_taps)
    skip = skip_gain.reshape(1, cols)
    place = places(seq)
    by_owner = pack((queries, keys, values), seq)
    x = lax.all_to_all(by_owner, "seq", split_axis=0, concat_axis=0, tiled=True)
    held = own_cotangent(cotangent, col_part, by_owner)
    tail = tail_of(x, short_taps, [fwd_table, held])
    halo = along(tail, fsdp, 1)
    cots = gather_cotangent(held, [halo])
    mixers = []
    for h in range(chunks):
        after = mixers[-1][0] if mixers else cots[0]
        mixers.append(forward(x, halo, short_taps, skip, fwd_table, place, h, chunks, after))

    mixed_all = [
        [around(mixed, "y", step) if step else mixed for step in range(ys)] for mixed, _, _ in mixers
    ]

    parts, heads = [], []
    for step in range(1, ys):
        part, head = mixed_grad(cots, weights, place, step, BF16, [parts[-1] if parts else mixers[-1][0]])
        parts.append(part)
        heads.append(around(head, "y", -step))
    mixed_own, own_head, parts[-1] = mixed_grad(
        cots, weights, place, 0, F32, [parts[-1], *[piece for pieces in mixed_all for piece in pieces[1:]]], True
    )
    rest = [around(parts[step - 1], "y", -step) for step in range(1, ys)]
    mixed_rest = rest[0] if len(rest) == 1 else sum(piece.astype(F32) for piece in rest)
    head_rest = heads[0] if len(heads) == 1 else sum(piece.astype(F32) for piece in heads)
    head = head_of(own_head, head_rest, mixers, [])
    later = along(head, fsdp, -1)

    weight_sum = None
    for h in range(chunks):
        after = [later] if h == chunks - 1 else [head]
        weight_sum = weight_grad(cots, mixed_all[h], h, chunks, grad_scale, weight_sum, after)
    weight_part = lax.psum_scatter(weight_sum, "z", scatter_dimension=1, tiled=True)

    grads, short_parts, long_parts = [], [], []
    for h in range(chunks):
        _, feats, filt = mixers[h]
        grad, short_part, long_part = backward(
            mixed_own, mixed_rest, feats, filt, x, later, short_taps, skip, bwd_table, h, chunks
        )
        grads.append(lax.all_to_all(grad, "seq", split_axis=0, concat_axis=0, tiled=True))
        short_parts.append(short_part)
        long_parts.append(long_part)

    query_grad, key_grad, value_grad = unpack(grads)
    packed = jnp.concatenate(
        [
            jnp.concatenate(short_parts, axis=2).reshape(3 * (SHORT + 1), cols),
            jnp.concatenate(long_parts, axis=0).reshape(-1, cols),
        ],
        axis=0,
    )
    packed = sum_over(packed, ("y", "z")) * grad_scale
    short_sum = packed[: 3 * (SHORT + 1)].reshape(3, SHORT + 1, cols)
    long_sum = packed[3 * (SHORT + 1) :].reshape(groups, LTAPS).T
    return (
        query_grad,
        key_grad,
        value_grad,
        weight_part.astype(F32),
        short_sum[:, :SHORT],
        long_sum,
        short_sum[0, SHORT],
    )


def solution(mesh):
    fsdp, seq = mesh.shape["fsdp"], mesh.shape["seq"]
    split = Mesh(mesh.devices.reshape(Z, fsdp // Z, seq), ("z", "y", "seq"))
    tokens = P(("z", "y", "seq"), None)
    specs = (P("seq", ("z", "y")), P(None, None, "seq"), P(None, "seq"), P("seq"))
    return jax.shard_map(
        body,
        mesh=split,
        in_specs=(tokens,) * 4 + specs,
        out_specs=(tokens,) * 3 + specs,
        check_vma=False,
    )
```

profile of v0, /device:TPU:0, one launch (start us, length us, event | category | flops | bytes accessed | tf_op | source)
XLA Modules:
  0.0 287.4 jit_solution(18311795587801407178)
XLA Ops:
  7.9 4.2 %pack.1.refs_2_ = bf16[4,3,128,1024]{3,2,1,0:T(8,128)(2,1)} custom-call(bf16[128,4096]{1,0:T(8,128)(2,1)} %refs_0_.2, bf16[128,4096]{1,0:T(8,128)(2,1)} %refs_1_.2, bf16[128,4096]{1,0:T(8,128)(2,1)} %refs_2_.1), custom_call_target="tpu_custom_call" | custom-call | tf_op jit(solution)/shard_map/pack/pallas_call | solution.py:282
  12.1 4.2 %all-to-all-start = ((bf16[4,3,128,1024]{3,2,1,0:T(8,128)(2,1)}), bf16[4,3,128,1024]{3,2,1,0:T(8,128)(2,1)S(1)}, u32[]{:S(2)}, u32[]{:S(2)}) async-start(bf16[4,3,128,1024]{3,2,1,0:T(8,128)(2,1)} %pack.1.refs_2_), calls=%async_computation | async-start | bytes 6291456 | tf_op jit(solution)/shard_map/all_to_all | solution.py:588
  16.3 3.5 %split.1 = (bf16[128,2048]{1,0:T(8,128)(2,1)}, bf16[128,2048]{1,0:T(8,128)(2,1)}) custom-call(s32[1]{0:T(128)} %bitcast.y_ref, bf16[128,4096]{1,0:T(8,128)(2,1)} %refs_1_.3, bf16[128,4096]{1,0:T(8,128)(2,1)} %refs_1_.3, bf16[4,3,128,1024]{3,2,1,0:T(8,128)(2,1)} %pack.1.refs_2_), custom_call_target="tpu_custom_call" | custom-call | tf_op jit(solution)/shard_map/split/pallas_call | solution.py:354
  22.3 12.7 %collective-permute-done = bf16[128,2048]{1,0:T(8,128)(2,1)S(1)} collective-permute-done((bf16[128,2048]{1,0:T(8,128)(2,1)}, bf16[128,2048]{1,0:T(8,128)(2,1)S(1)}, u32[]{:S(2)}, u32[]{:S(2)}) %collective-permute-start) | collective-permute-done | bytes 524320 | tf_op jit(solution)/shard_map/ppermute | solution.py:323
  35.8 3.4 %join.2.refs_1_.refs_0_ = bf16[2,1,128,2048]{3,2,1,0:T(8,128)(2,1)} custom-call(bf16[1,1,128,2048]{3,2,1,0:T(8,128)(2,1)} %bitcast.12, bf16[1,1,128,2048]{3,2,1,0:T(8,128)(2,1)} %bitcast.13), custom_call_target="tpu_custom_call" | custom-call | tf_op jit(solution)/shard_map/join/pallas_call | solution.py:384
  42.3 6.7 %tables.1 = (bf16[8192,256]{1,0:T(8,128)(2,1)}, bf16[8192,256]{1,0:T(8,128)(2,1)}) custom-call(f32[64,256]{1,0:T(8,128)} %pad.8.fwd_ref, f32[64,256]{1,0:T(8,128)} %pad.9.bwd_ref), custom_call_target="tpu_custom_call" | custom-call | tf_op jit(solution)/shard_map/tables/pallas_call | solution.py:41
  49.0 5.2 %all-to-all-done.x_ref.before_ref = bf16[4,3,128,1024]{3,2,1,0:T(8,128)(2,1)S(1)} async-done(((bf16[4,3,128,1024]{3,2,1,0:T(8,128)(2,1)}), bf16[4,3,128,1024]{3,2,1,0:T(8,128)(2,1)S(1)}, u32[]{:S(2)}, u32[]{:S(2)}) %all-to-all-start) | async-done | bytes 3145760 | tf_op jit(solution)/shard_map/all_to_all | solution.py:588
  58.1 3.9 %collective-permute-start.2 = (bf16[176,1024]{1,0:T(8,128)(2,1)}, bf16[176,1024]{1,0:T(8,128)(2,1)S(1)}, u32[]{:S(2)}, u32[]{:S(2)}) collective-permute-start(bf16[176,1024]{1,0:T(8,128)(2,1)} %tail.1), channel_id=1, source_target_pairs={{0,4},{4,8},{8,12},{12,16},{16,20},{20,24},{24,28},{1,5},{5,9},{9,... | collective-permute-start | bytes 1081352 | tf_op jit(solution)/shard_map/ppermute | solution.py:318
  62.0 13.9 %collective-permute-done.1.refs_1_ = bf16[2,1,128,2048]{3,2,1,0:T(8,128)(2,1)} collective-permute-done((bf16[2,1,128,2048]{3,2,1,0:T(8,128)(2,1)}, bf16[2,1,128,2048]{3,2,1,0:T(8,128)(2,1)}, u32[]{:S(2)}, u32[]{:S(2)}) %collective-permute-start.1) | collective-permute-done | bytes 1048608 | tf_op jit(solution)/shard_map/ppermute | solution.py:327
  76.6 3.8 %join.3._.a_ref = bf16[2,2,128,2048]{3,2,1,0:T(8,128)(2,1)} custom-call(bf16[2,1,128,2048]{3,2,1,0:T(8,128)(2,1)} %join.2.refs_1_.refs_0_, bf16[2,1,128,2048]{3,2,1,0:T(8,128)(2,1)} %collective-permute-done.1.refs_1_, bf16[176,1024]{1,0:T(8,128)(2,1)} %copy-done.4), custom_call_target="tpu_custom_call" | custom-call | tf_op jit(solution)/shard_map/join/pallas_call | solution.py:384
  80.9 7.4 %forward.2 = (bf16[512,512]{1,0:T(8,128)(2,1)}, f32[3,512,512]{2,1,0:T(8,128)}, f32[512,512]{1,0:T(8,128)}) custom-call(s32[4]{0:T(128)} %shift-left_add_fusion.place_ref, bf16[4,3,128,1024]{3,2,1,0:T(8,128)(2,1)} %copy-done, bf16[176,1024]{1,0:T(8,128)(2,1)} %copy-done.4, f32[3,7,1024]{2,1,0:T(8,128)} %taps_ref.9, f32[1,1024]{1,0:T(1,128)} %bitcast.18, ...), custom_call_target="tpu_custom_call" | custom-call | tf_op jit(solution)/shard_map/forward/pallas_call | solution.py:111
  88.3 7.5 %forward.3 = (bf16[512,512]{1,0:T(8,128)(2,1)}, f32[3,512,512]{2,1,0:T(8,128)}, f32[512,512]{1,0:T(8,128)}) custom-call(s32[4]{0:T(128)} %shift-left_add_fusion.place_ref, bf16[4,3,128,1024]{3,2,1,0:T(8,128)(2,1)} %copy-done, bf16[176,1024]{1,0:T(8,128)(2,1)} %copy-done.4, f32[3,7,1024]{2,1,0:T(8,128)} %taps_ref.9, f32[1,1024]{1,0:T(1,128)} %bitcast.19, ...), custom_call_target="tpu_custom_call" | custom-call | tf_op jit(solution)/shard_map/forward/pallas_call | solution.py:111
  95.9 3.8 %collective-permute-start.5 = (bf16[512,512]{1,0:T(8,128)(2,1)}, bf16[512,512]{1,0:T(8,128)(2,1)}, u32[]{:S(2)}, u32[]{:S(2)}) collective-permute-start(bf16[512,512]{1,0:T(8,128)(2,1)} %get-tuple-element.35.refs_0_), channel_id=1, source_target_pairs={{0,4},{4,0},{1,5},{5,1},{2,6},{6,2},{3,7},{7,3},{8,12},{12,8},{9,1... | collective-permute-start | bytes 1572872 | tf_op jit(solution)/shard_map/ppermute | solution.py:323
  101.2 7.0 %mixed_grad.2 = (bf16[512,1024]{1,0:T(8,128)(2,1)}, bf16[144,1024]{1,0:T(8,128)(2,1)}) custom-call(s32[4]{0:T(128)} %shift-left_add_fusion.place_ref, bf16[2,2,128,2048]{3,2,1,0:T(8,128)(2,1)} %join.3._.a_ref, bf16[2,2,128,2048]{3,2,1,0:T(8,128)(2,1)} %copy-done.1, bf16[1024,2048]{1,0:T(8,128)(2,1)} %all-gather.2.cloned.1.call-done.w_ref, ...), custom_call_target="tpu_custom_call" | custom-call | tf_op jit(solution)/shard_map/mixed_grad/pallas_call | solution.py:428
  108.2 4.5 %collective-permute-done.5.refs_2_.refs_1_ = bf16[512,512]{1,0:T(8,128)(2,1)} collective-permute-done((bf16[512,512]{1,0:T(8,128)(2,1)}, bf16[512,512]{1,0:T(8,128)(2,1)}, u32[]{:S(2)}, u32[]{:S(2)}) %collective-permute-start.5) | collective-permute-done | bytes 524320 | tf_op jit(solution)/shard_map/ppermute | solution.py:323
  112.8 10.9 %collective-permute-done.4.refs_1_ = bf16[512,512]{1,0:T(8,128)(2,1)S(1)} collective-permute-done((bf16[512,512]{1,0:T(8,128)(2,1)S(1)}, bf16[512,512]{1,0:T(8,128)(2,1)S(1)}, u32[]{:S(2)}, u32[]{:S(2)}) %collective-permute-start.4) | collective-permute-done | bytes 524320 | tf_op jit(solution)/shard_map/ppermute | solution.py:323
  124.6 7.5 %mixed_grad.3 = (f32[512,1024]{1,0:T(8,128)}, f32[144,1024]{1,0:T(8,128)}, bf16[512,1024]{1,0:T(8,128)(2,1)}) custom-call(s32[4]{0:T(128)} %shift-left_add_fusion.place_ref, bf16[2,2,128,2048]{3,2,1,0:T(8,128)(2,1)} %join.3._.a_ref, bf16[2,2,128,2048]{3,2,1,0:T(8,128)(2,1)} %copy-done.1, ...), custom_call_target="tpu_custom_call", output_to_operand_aliasing={{2}: (4, {})} | custom-call | tf_op jit(solution)/shard_map/mixed_grad/pallas_call | solution.py:428
  134.1 29.5 %collective-permute-done.7.mr_ref = bf16[144,1024]{1,0:T(8,128)(2,1)S(1)} collective-permute-done((bf16[144,1024]{1,0:T(8,128)(2,1)S(1)}, bf16[144,1024]{1,0:T(8,128)(2,1)S(1)}, u32[]{:S(2)}, u32[]{:S(2)}) %collective-permute-start.7) | collective-permute-done | bytes 294944 | tf_op jit(solution)/shard_map/ppermute | solution.py:323
  168.3 6.0 %weight_grad.2.refs_3_ = bf16[1024,2048]{1,0:T(8,128)(2,1)} custom-call(bf16[2,2,128,2048]{3,2,1,0:T(8,128)(2,1)} %join.3._.a_ref, bf16[2,2,128,2048]{3,2,1,0:T(8,128)(2,1)} %copy-done.1, bf16[512,512]{1,0:T(8,128)(2,1)} %get-tuple-element.34._.refs_0_, bf16[512,512]{1,0:T(8,128)(2,1)} %copy-done.6, bf16[192,1024]{1,0:T(8,128)(2,1)} %head.1.refs_2_), custom_call_target="tpu_custom_call" | custom-call | tf_op jit(solution)/shard_map/weight_grad/pallas_call | solution.py:476
  174.3 4.9 %collective-permute-done.8.n_ref.refs_2_ = bf16[192,1024]{1,0:T(8,128)(2,1)S(1)} collective-permute-done((bf16[192,1024]{1,0:T(8,128)(2,1)}, bf16[192,1024]{1,0:T(8,128)(2,1)S(1)}, u32[]{:S(2)}, u32[]{:S(2)}) %collective-permute-start.8) | collective-permute-done | bytes 393248 | tf_op jit(solution)/shard_map/ppermute | solution.py:318
  179.9 6.1 %weight_grad.3 = bf16[1024,2048]{1,0:T(8,128)(2,1)} custom-call(bf16[2,2,128,2048]{3,2,1,0:T(8,128)(2,1)} %join.3._.a_ref, bf16[2,2,128,2048]{3,2,1,0:T(8,128)(2,1)} %copy-done.1, bf16[512,512]{1,0:T(8,128)(2,1)} %get-tuple-element.35.refs_0_, bf16[512,512]{1,0:T(8,128)(2,1)} %collective-permute-done.5.refs_2_.refs_1_, ...), custom_call_target="tpu_custom_call", output_to_operand_aliasing={{}: (5, {})} | custom-call | tf_op jit(solution)/shard_map/weight_grad/pallas_call | solution.py:476
  187.0 10.6 %backward.3 = (bf16[4,3,128,512]{3,2,1,0:T(8,128)(2,1)}, f32[3,8,512]{2,1,0:T(8,128)}, f32[32,128]{1,0:T(8,128)}) custom-call(f32[512,1024]{1,0:T(8,128)} %get-tuple-element.37.mo_ref, bf16[512,1024]{1,0:T(8,128)(2,1)} %copy-done.14, f32[3,512,512]{2,1,0:T(8,128)} %get-tuple-element.43.refs_2_.f_ref, f32[512,512]{1,0:T(8,128)} %get-tuple-element.44.refs_3_.filt_ref, ...), custom_call_target="tpu_custom_call" | custom-call | flops 99999997952 | bytes 9437184 | tf_op jit(solution)/shard_map/backward/pallas_call | solution.py:236
  197.6 3.6 %all-to-all-start.2 = ((bf16[4,3,128,512]{3,2,1,0:T(8,128)(2,1)}), bf16[4,3,128,512]{3,2,1,0:T(8,128)(2,1)S(1)}, u32[]{:S(2)}, u32[]{:S(2)}) async-start(bf16[4,3,128,512]{3,2,1,0:T(8,128)(2,1)} %get-tuple-element.47), calls=%async_computation.2 | async-start | bytes 3145728 | tf_op jit(solution)/shard_map/all_to_all | solution.py:628
  201.2 10.8 %backward.2 = (bf16[4,3,128,512]{3,2,1,0:T(8,128)(2,1)}, f32[3,8,512]{2,1,0:T(8,128)}, f32[32,128]{1,0:T(8,128)}) custom-call(f32[512,1024]{1,0:T(8,128)} %get-tuple-element.37.mo_ref, bf16[512,1024]{1,0:T(8,128)(2,1)} %copy-done.14, f32[3,512,512]{2,1,0:T(8,128)} %get-tuple-element.39.refs_0_.f_ref, f32[512,512]{1,0:T(8,128)} %get-tuple-element.40.refs_1_.filt_ref, ...), custom_call_target="tpu_custom_call" | custom-call | flops 99999997952 | bytes 9437184 | tf_op jit(solution)/shard_map/backward/pallas_call | solution.py:236
  213.6 7.6 %all-to-all-done.2.refs_1_ = bf16[4,3,128,512]{3,2,1,0:T(8,128)(2,1)S(1)} async-done(((bf16[4,3,128,512]{3,2,1,0:T(8,128)(2,1)}), bf16[4,3,128,512]{3,2,1,0:T(8,128)(2,1)S(1)}, u32[]{:S(2)}, u32[]{:S(2)}) %all-to-all-start.2) | async-done | bytes 1572896 | tf_op jit(solution)/shard_map/all_to_all | solution.py:628
  221.2 3.6 %all-to-all-start.1 = ((bf16[4,3,128,512]{3,2,1,0:T(8,128)(2,1)}), bf16[4,3,128,512]{3,2,1,0:T(8,128)(2,1)S(1)}, u32[]{:S(2)}, u32[]{:S(2)}) async-start(bf16[4,3,128,512]{3,2,1,0:T(8,128)(2,1)} %get-tuple-element.46), calls=%async_computation.1 | async-start | bytes 3145728 | tf_op jit(solution)/shard_map/all_to_all | solution.py:628
  224.8 8.4 %collective-permute-start.9 = (f32[32,1024]{1,0:T(8,128)S(1)}, f32[32,1024]{1,0:T(8,128)S(1)}, u32[]{:S(2)}, u32[]{:S(2)}) collective-permute-start(f32[32,1024]{1,0:T(8,128)S(1)} %pad_maximum_fusion), channel_id=1, source_target_pairs={{0,4},{4,0},{1,5},{5,1},{2,6},{6,2},{3,7},{7,3},{8,12},{12,8},{9,1... | collective-permute-start | bytes 393224 | tf_op jit(solution)/shard_map/ppermute | solution.py:327
  233.2 4.1 %collective-permute-done.9 = f32[32,1024]{1,0:T(8,128)S(1)} collective-permute-done((f32[32,1024]{1,0:T(8,128)S(1)}, f32[32,1024]{1,0:T(8,128)S(1)}, u32[]{:S(2)}, u32[]{:S(2)}) %collective-permute-start.9) | collective-permute-done | bytes 131104 | tf_op jit(solution)/shard_map/ppermute | solution.py:327
  240.7 10.0 %collective-permute-done.10 = f32[32,1024]{1,0:T(8,128)S(1)} collective-permute-done((f32[32,1024]{1,0:T(8,128)S(1)}, f32[32,1024]{1,0:T(8,128)S(1)}, u32[]{:S(2)}, u32[]{:S(2)}) %collective-permute-start.10) | collective-permute-done | bytes 131104 | tf_op jit(solution)/shard_map/ppermute | solution.py:327
  250.7 3.7 %collective-permute-start.11 = (f32[32,1024]{1,0:T(8,128)S(1)}, f32[32,1024]{1,0:T(8,128)S(1)}, u32[]{:S(2)}, u32[]{:S(2)}) collective-permute-start(f32[32,1024]{1,0:T(8,128)S(1)} %add.20), channel_id=1, source_target_pairs={{0,16},{8,24},{16,0},{24,8},{1,17},{9,25},{17,1},{25,9},{2,18},{10... | collective-permute-start | bytes 393224 | tf_op jit(solution)/shard_map/ppermute | solution.py:327
  254.4 15.9 %collective-permute-done.11 = f32[32,1024]{1,0:T(8,128)S(1)} collective-permute-done((f32[32,1024]{1,0:T(8,128)S(1)}, f32[32,1024]{1,0:T(8,128)S(1)}, u32[]{:S(2)}, u32[]{:S(2)}) %collective-permute-start.11) | collective-permute-done | bytes 131104 | tf_op jit(solution)/shard_map/ppermute | solution.py:327
  272.8 4.2 %unpack.1 = (bf16[128,4096]{1,0:T(8,128)(2,1)}, bf16[128,4096]{1,0:T(8,128)(2,1)}, bf16[128,4096]{1,0:T(8,128)(2,1)}) custom-call(bf16[4,3,128,512]{3,2,1,0:T(8,128)(2,1)} %copy-done.3, bf16[4,3,128,512]{3,2,1,0:T(8,128)(2,1)} %copy-done.2), custom_call_target="tpu_custom_call" | custom-call | tf_op jit(solution)/shard_map/unpack/pallas_call | solution.py:305
  (68 shorter events, 34.2 us)
Async XLA Ops:
  7.2 92.6 %all-gather.2.cloned.1.call-start = ((), (), s32[]{:S(2)}) async-start(), calls=%async_computation.4 | async-start | bytes 5242880 | tf_op jit(solution)/shard_map/all_gather | solution.py:583
  12.1 42.0 %all-to-all-start = ((bf16[4,3,128,1024]{3,2,1,0:T(8,128)(2,1)}), bf16[4,3,128,1024]{3,2,1,0:T(8,128)(2,1)S(1)}, u32[]{:S(2)}, u32[]{:S(2)}) async-start(bf16[4,3,128,1024]{3,2,1,0:T(8,128)(2,1)} %pack.1.refs_2_), calls=%async_computation | async-start | bytes 6291456 | tf_op jit(solution)/shard_map/all_to_all | solution.py:588
  16.3 261.4 %reduce-scatter.2.cloned.1.call-start = ((), (), s32[]{:S(2)}) async-start(), calls=%async_computation.5 | async-start | bytes 5242880 | tf_op jit(solution)/shard_map/reduce_scatter | solution.py:620
  16.3 24.6 %copy-start.10 = (f32[128,64]{0,1:T(8,128)S(1)}, f32[128,64]{0,1:T(8,128)}, u32[]{:S(2)}) copy-start(f32[128,64]{0,1:T(8,128)} %param.14) | copy-start | bytes 98308
  19.8 15.2 %collective-permute-start = (bf16[128,2048]{1,0:T(8,128)(2,1)}, bf16[128,2048]{1,0:T(8,128)(2,1)S(1)}, u32[]{:S(2)}, u32[]{:S(2)}) collective-permute-start(bf16[128,2048]{1,0:T(8,128)(2,1)} %get-tuple-element.32), channel_id=1, source_target_pairs={{0,4},{4,0},{1,5},{5,1},{2,6},{6,2},{3,7},{7,3},{8,12},{12,8},{9,1... | collective-permute-start | bytes 1572872 | tf_op jit(solution)/shard_map/ppermute | solution.py:323
  35.0 0.8 copy-start.7
  39.2 36.7 %collective-permute-start.1 = (bf16[2,1,128,2048]{3,2,1,0:T(8,128)(2,1)}, bf16[2,1,128,2048]{3,2,1,0:T(8,128)(2,1)}, u32[]{:S(2)}, u32[]{:S(2)}) collective-permute-start(bf16[2,1,128,2048]{3,2,1,0:T(8,128)(2,1)} %join.2.refs_1_.refs_0_), channel_id=1, source_target_pairs={{0,2},{1,3},{2,0},{3,1},{4,6},{5,7},{6,4},{7,5},{8,10},{9,11},{10,... | collective-permute-start | bytes 3145736 | tf_op jit(solution)/shard_map/ppermute | solution.py:327
  54.2 1.6 copy-start
  58.1 17.8 %collective-permute-start.2 = (bf16[176,1024]{1,0:T(8,128)(2,1)}, bf16[176,1024]{1,0:T(8,128)(2,1)S(1)}, u32[]{:S(2)}, u32[]{:S(2)}) collective-permute-start(bf16[176,1024]{1,0:T(8,128)(2,1)} %tail.1), channel_id=1, source_target_pairs={{0,4},{4,8},{8,12},{12,16},{16,20},{20,24},{24,28},{1,5},{5,9},{9,... | collective-permute-start | bytes 1081352 | tf_op jit(solution)/shard_map/ppermute | solution.py:318
  75.9 0.7 copy-start.4
  80.4 19.4 %collective-permute-start.3 = (bf16[2,2,128,2048]{3,2,1,0:T(8,128)(2,1)}, bf16[2,2,128,2048]{3,2,1,0:T(8,128)(2,1)S(1)}, u32[]{:S(2)}, u32[]{:S(2)}) collective-permute-start(bf16[2,2,128,2048]{3,2,1,0:T(8,128)(2,1)} %join.3._.a_ref), channel_id=1, source_target_pairs={{0,1},{1,0},{2,3},{3,2},{4,5},{5,4},{6,7},{7,6},{8,9},{9,8},{10,11... | collective-permute-start | bytes 6291464 | tf_op jit(solution)/shard_map/ppermute | solution.py:327
  88.3 11.4 %copy-start.5 = (bf16[512,512]{1,0:T(8,128)(2,1)S(1)}, bf16[512,512]{1,0:T(8,128)(2,1)}, u32[]{:S(2)}) copy-start(bf16[512,512]{1,0:T(8,128)(2,1)} %get-tuple-element.34._.refs_0_) | copy-start | bytes 1572868
  95.9 16.9 %collective-permute-start.5 = (bf16[512,512]{1,0:T(8,128)(2,1)}, bf16[512,512]{1,0:T(8,128)(2,1)}, u32[]{:S(2)}, u32[]{:S(2)}) collective-permute-start(bf16[512,512]{1,0:T(8,128)(2,1)} %get-tuple-element.35.refs_0_), channel_id=1, source_target_pairs={{0,4},{4,0},{1,5},{5,1},{2,6},{6,2},{3,7},{7,3},{8,12},{12,8},{9,1... | collective-permute-start | bytes 1572872 | tf_op jit(solution)/shard_map/ppermute | solution.py:323
  99.7 24.0 %collective-permute-start.4 = (bf16[512,512]{1,0:T(8,128)(2,1)S(1)}, bf16[512,512]{1,0:T(8,128)(2,1)S(1)}, u32[]{:S(2)}, u32[]{:S(2)}) collective-permute-start(bf16[512,512]{1,0:T(8,128)(2,1)S(1)} %copy-done.5), channel_id=1, source_target_pairs={{0,4},{4,0},{1,5},{5,1},{2,6},{6,2},{3,7},{7,3},{8,12},{12,8},{9,1... | collective-permute-start | bytes 1572872 | tf_op jit(solution)/shard_map/ppermute | solution.py:323
  99.8 1.4 copy-start.1
  123.7 0.8 copy-start.6
  124.6 9.2 %copy-start.15 = (bf16[144,1024]{1,0:T(8,128)(2,1)S(1)}, bf16[144,1024]{1,0:T(8,128)(2,1)}, u32[]{:S(2)}) copy-start(bf16[144,1024]{1,0:T(8,128)(2,1)} %get-tuple-element.42) | copy-start | bytes 884740
  132.1 54.0 %collective-permute-start.6 = (bf16[512,1024]{1,0:T(8,128)(2,1)}, bf16[512,1024]{1,0:T(8,128)(2,1)S(1)}, u32[]{:S(2)}, u32[]{:S(2)}) collective-permute-start(bf16[512,1024]{1,0:T(8,128)(2,1)} %get-tuple-element.38), channel_id=1, source_target_pairs={{0,4},{4,0},{1,5},{5,1},{2,6},{6,2},{3,7},{7,3},{8,12},{12,8},{9,1... | collective-permute-start | bytes 3145736 | tf_op jit(solution)/shard_map/ppermute | solution.py:323
  133.8 29.8 %collective-permute-start.7 = (bf16[144,1024]{1,0:T(8,128)(2,1)S(1)}, bf16[144,1024]{1,0:T(8,128)(2,1)S(1)}, u32[]{:S(2)}, u32[]{:S(2)}) collective-permute-start(bf16[144,1024]{1,0:T(8,128)(2,1)S(1)} %copy-done.15), channel_id=1, source_target_pairs={{0,4},{4,0},{1,5},{5,1},{2,6},{6,2},{3,7},{7,3},{8,12},{12,8},{9,1... | collective-permute-start | bytes 884744 | tf_op jit(solution)/shard_map/ppermute | solution.py:323
  167.0 12.2 %collective-permute-start.8 = (bf16[192,1024]{1,0:T(8,128)(2,1)}, bf16[192,1024]{1,0:T(8,128)(2,1)S(1)}, u32[]{:S(2)}, u32[]{:S(2)}) collective-permute-start(bf16[192,1024]{1,0:T(8,128)(2,1)} %head.1.refs_2_), channel_id=1, source_target_pairs={{4,0},{8,4},{12,8},{16,12},{20,16},{24,20},{28,24},{5,1},{9,5},{13... | collective-permute-start | bytes 1179656 | tf_op jit(solution)/shard_map/ppermute | solution.py:318
  179.2 0.8 copy-start.8
  186.0 1.0 copy-start.14
  197.6 23.6 %all-to-all-start.2 = ((bf16[4,3,128,512]{3,2,1,0:T(8,128)(2,1)}), bf16[4,3,128,512]{3,2,1,0:T(8,128)(2,1)S(1)}, u32[]{:S(2)}, u32[]{:S(2)}) async-start(bf16[4,3,128,512]{3,2,1,0:T(8,128)(2,1)} %get-tuple-element.47), calls=%async_computation.2 | async-start | bytes 3145728 | tf_op jit(solution)/shard_map/all_to_all | solution.py:628
  201.2 10.9 %copy-start.13 = (f32[32,128]{1,0:T(8,128)S(1)}, f32[32,128]{1,0:T(8,128)}, u32[]{:S(2)}) copy-start(f32[32,128]{1,0:T(8,128)} %get-tuple-element.54) | copy-start | bytes 49156
  201.2 11.6 %copy-start.12 = (f32[3,8,512]{2,1,0:T(8,128)S(1)}, f32[3,8,512]{2,1,0:T(8,128)}, u32[]{:S(2)}) copy-start(f32[3,8,512]{2,1,0:T(8,128)} %get-tuple-element.52) | copy-start | bytes 147460
  221.2 50.4 %copy-start.2 = (bf16[4,3,128,512]{3,2,1,0:T(8,128)(2,1)}, bf16[4,3,128,512]{3,2,1,0:T(8,128)(2,1)S(1)}, u32[]{:S(2)}) copy-start(bf16[4,3,128,512]{3,2,1,0:T(8,128)(2,1)S(1)} %all-to-all-done.2.refs_1_) | copy-start | bytes 4718596
  221.2 50.4 %all-to-all-start.1 = ((bf16[4,3,128,512]{3,2,1,0:T(8,128)(2,1)}), bf16[4,3,128,512]{3,2,1,0:T(8,128)(2,1)S(1)}, u32[]{:S(2)}, u32[]{:S(2)}) async-start(bf16[4,3,128,512]{3,2,1,0:T(8,128)(2,1)} %get-tuple-element.46), calls=%async_computation.1 | async-start | bytes 3145728 | tf_op jit(solution)/shard_map/all_to_all | solution.py:628
  224.8 12.5 %collective-permute-start.9 = (f32[32,1024]{1,0:T(8,128)S(1)}, f32[32,1024]{1,0:T(8,128)S(1)}, u32[]{:S(2)}, u32[]{:S(2)}) collective-permute-start(f32[32,1024]{1,0:T(8,128)S(1)} %pad_maximum_fusion), channel_id=1, source_target_pairs={{0,4},{4,0},{1,5},{5,1},{2,6},{6,2},{3,7},{7,3},{8,12},{12,8},{9,1... | collective-permute-start | bytes 393224 | tf_op jit(solution)/shard_map/ppermute | solution.py:327
  237.4 13.4 %collective-permute-start.10 = (f32[32,1024]{1,0:T(8,128)S(1)}, f32[32,1024]{1,0:T(8,128)S(1)}, u32[]{:S(2)}, u32[]{:S(2)}) collective-permute-start(f32[32,1024]{1,0:T(8,128)S(1)} %fusion), channel_id=1, source_target_pairs={{0,8},{8,0},{16,24},{24,16},{1,9},{9,1},{17,25},{25,17},{2,10},{10... | collective-permute-start | bytes 393224 | tf_op jit(solution)/shard_map/ppermute | solution.py:327
  250.7 19.6 %collective-permute-start.11 = (f32[32,1024]{1,0:T(8,128)S(1)}, f32[32,1024]{1,0:T(8,128)S(1)}, u32[]{:S(2)}, u32[]{:S(2)}) collective-permute-start(f32[32,1024]{1,0:T(8,128)S(1)} %add.20), channel_id=1, source_target_pairs={{0,16},{8,24},{16,0},{24,8},{1,17},{9,25},{17,1},{25,9},{2,18},{10... | collective-permute-start | bytes 393224 | tf_op jit(solution)/shard_map/ppermute | solution.py:327
  271.0 9.6 %copy-start.11 = (f32[3,8,1024]{2,1,0:T(8,128)}, f32[3,8,1024]{2,1,0:T(8,128)S(1)}, u32[]{:S(2)}) copy-start(f32[3,8,1024]{2,1,0:T(8,128)S(1)} %slice_bitcast_fusion) | copy-start | bytes 294916
  271.6 1.1 copy-start.3
  (1 other events, 0.7 us)
Sparse Core Ops, SparseCore 0:
  9.6 83.4 all-gather.1
  186.2 91.5 reduce-scatter.1
where the time goes:
time: 289 us; the launch traced here: 287 us
  waiting for transfers between devices  121 us (42%)
  Pallas kernels  93.6 us (32%)
  starting transfers between devices  42.1 us (15%)
  between operations  14.2 us (5%)
  local copies, waits for them, and re-layouts  11.7 us (4%)
  other arithmetic  4.95 us (2%)
    ppermute x5, waiting for transfers between devices, around(): lax.ppermute(block, axis, [(i, (i + distance) % size) for i in range(size)])  57.7 us
    ppermute x5, waiting for transfers between devices, across(): lax.ppermute(block, axis, [(i, i ^ bit) for i in range(lax.axis_size(axis...  43.9 us
    pallas_call x2, Pallas kernels, backward(): pl.pallas_call(backward_kernel, grid=(tiles,), in_specs=[tok, tok, pl.Blo...  21.4 us
    ppermute x5, starting transfers between devices, across(): lax.ppermute(block, axis, [(i, i ^ bit) for i in range(lax.axis_size(axis...  17.1 us
    pallas_call x2, Pallas kernels, forward(): pl.pallas_call(forward_kernel, grid_spec=pltpu.PrefetchScalarGridSpec(num...  14.9 us
    pallas_call x2, Pallas kernels, mixed_grad(): pl.pallas_call(functools.partial(mixed_grad_kernel, len(after)), grid_spe...  14.5 us
    pallas_call x2, Pallas kernels, weight_grad(): pl.pallas_call(functools.partial(weight_grad_kernel, scale), grid=(Z,), i...  12.1 us
    unnamed x32, local copies, waits for them, and re-layouts  9.02 us
  transfers between devices with their start and end apart: 17, of which 12 were waited for; matrix products, arithmetic and copies ran while one was open for 2% of the time, Pallas kernels for 30%

commit v1 on v0

--- a/solution.py
+++ b/solution.py
@@ -419,7 +419,7 @@
     head_ref[...] = out_ref[0 : LTAPS + PAD]
 
 
-def mixed_grad(cots, weights, place, step, dtype, after, passed=False):
+def mixed_grad(cots, weights, place, step, dtype, after):
     _, count, rows, width = cots[0].shape
     tokens = 2 * count * rows
     cols = weights.shape[0]
@@ -439,16 +439,13 @@
             out_specs=[
                 pl.BlockSpec((tokens, tile), lambda i, _: (0, i)),
                 pl.BlockSpec((LTAPS + PAD, tile), lambda i, _: (0, i)),
-            ]
-            + [pl.BlockSpec(memory_space=pl.ANY)] * passed,
+            ],
             scratch_shapes=[pltpu.VMEM((tokens, tile), F32)],
         ),
-        input_output_aliases={4: 2} if passed else {},
         out_shape=[
             jax.ShapeDtypeStruct((tokens, cols), dtype),
             jax.ShapeDtypeStruct((LTAPS + PAD, cols), dtype),
-        ]
-        + [jax.ShapeDtypeStruct(after[0].shape, after[0].dtype)] * passed,
+        ],
         compiler_params=params(),
         name="mixed_grad",
     )(place, *cots, weights, *after)
@@ -528,7 +525,7 @@
 
 
 def head_kernel(chunks, mo_ref, mr_ref, *refs):
-    out_ref = refs[-1]
+    out_ref = refs[-2]
     edge = LTAPS + PAD
     part = out_ref.shape[1] // chunks
     for h in range(chunks):
@@ -541,7 +538,7 @@
         out_ref[edge + 2 * PAD :, own] = (mixed[0:PAD] * filt_ref[0:PAD]).astype(BF16)
 
 
-def head_of(mixed_own, mixed_rest, mixers, after):
+def head_of(mixed_own, mixed_rest, mixers, passed):
     edge, cols = LTAPS + PAD, mixed_own.shape[1]
     part = cols // len(mixers)
     whole = pl.BlockSpec((edge, cols), lambda i: (0, 0))
@@ -552,12 +549,16 @@
     return pl.pallas_call(
         functools.partial(head_kernel, len(mixers)),
         grid=(1,),
-        in_specs=[whole, whole] + feat_specs * len(mixers) + [pl.BlockSpec(memory_space=pl.ANY)] * len(after),
-        out_specs=pl.BlockSpec((edge + 3 * PAD, cols), lambda i: (0, 0)),
-        out_shape=jax.ShapeDtypeStruct((edge + 3 * PAD, cols), BF16),
+        in_specs=[whole, whole] + feat_specs * len(mixers) + [pl.BlockSpec(memory_space=pl.ANY)],
+        out_specs=[pl.BlockSpec((edge + 3 * PAD, cols), lambda i: (0, 0)), pl.BlockSpec(memory_space=pl.ANY)],
+        out_shape=[
+            jax.ShapeDtypeStruct((edge + 3 * PAD, cols), BF16),
+            jax.ShapeDtypeStruct(passed.shape, passed.dtype),
+        ],
+        input_output_aliases={2 + 2 * len(mixers): 1},
         compiler_params=params(),
         name="head",
-    )(mixed_own, mixed_rest, *[array for mixer in mixers for array in mixer[1:]], *after)
+    )(mixed_own, mixed_rest, *[array for mixer in mixers for array in mixer[1:]], passed)
 
 
 def contract(a, b, dim):
@@ -604,13 +605,11 @@
         part, head = mixed_grad(cots, weights, place, step, BF16, [parts[-1] if parts else mixers[-1][0]])
         parts.append(part)
         heads.append(around(head, "y", -step))
-    mixed_own, own_head, parts[-1] = mixed_grad(
-        cots, weights, place, 0, F32, [parts[-1], *[piece for pieces in mixed_all for piece in pieces[1:]]], True
-    )
+    mixed_own, own_head = mixed_grad(cots, weights, place, 0, F32, [parts[-1], *mixed_all[0][1:]])
+    head_rest = heads[0] if len(heads) == 1 else sum(piece.astype(F32) for piece in heads)
+    head, parts[-1] = head_of(own_head, head_rest, mixers, parts[-1])
     rest = [around(parts[step - 1], "y", -step) for step in range(1, ys)]
     mixed_rest = rest[0] if len(rest) == 1 else sum(piece.astype(F32) for piece in rest)
-    head_rest = heads[0] if len(heads) == 1 else sum(piece.astype(F32) for piece in heads)
-    head = head_of(own_head, head_rest, mixers, [])
     later = along(head, fsdp, -1)
 
     weight_sum = None

time: 289 us -> 275 us (0.952)
  waiting for transfers between devices: 121 us -> 107 us
    ppermute x5, waiting for transfers between devices: 57.7 us -> 47.8 us  [around(): lax.ppermute(block, axis, [(i, (i + distance) % size) for i in range(size)])]
    ppermute x2, waiting for transfers between devices: 4.87 us -> 1.09 us  [along(): lax.ppermute(block, axis, [(i, i + distance) for i in range(size) if 0 <=...]
  transfers between devices with their start and end apart: 17 -> 17, of which waited for: 12 -> 11; matrix products, arithmetic and copies ran while one was open for 2% -> 2% of each run, Pallas kernels for 30% -> 33%
where the time goes in v1:
time: 275 us; the launch traced here: 273 us
  waiting for transfers between devices  107 us (39%)
  Pallas kernels  93.4 us (34%)
  starting transfers between devices  41.7 us (15%)
  between operations  14.2 us (5%)
  local copies, waits for them, and re-layouts  11.6 us (4%)
  other arithmetic  4.95 us (2%)
    ppermute x5, waiting for transfers between devices, around(): lax.ppermute(block, axis, [(i, (i + distance) % size) for i in range(size)])  47.8 us
    ppermute x5, waiting for transfers between devices, across(): lax.ppermute(block, axis, [(i, i ^ bit) for i in range(lax.axis_size(axis...  44.3 us
    pallas_call x2, Pallas kernels, backward(): pl.pallas_call(backward_kernel, grid=(tiles,), in_specs=[tok, tok, pl.Blo...  21.4 us
    ppermute x5, starting transfers between devices, across(): lax.ppermute(block, axis, [(i, i ^ bit) for i in range(lax.axis_size(axis...  16.7 us
    pallas_call x2, Pallas kernels, forward(): pl.pallas_call(forward_kernel, grid_spec=pltpu.PrefetchScalarGridSpec(num...  14.8 us
    pallas_call x2, Pallas kernels, mixed_grad(): pl.pallas_call(functools.partial(mixed_grad_kernel, len(after)), grid_spe...  14.4 us
    pallas_call x2, Pallas kernels, weight_grad(): pl.pallas_call(functools.partial(weight_grad_kernel, scale), grid=(Z,), i...  12.1 us
    unnamed x32, local copies, waits for them, and re-layouts  8.93 us
  transfers between devices with their start and end apart: 17, of which 11 were waited for; matrix products, arithmetic and copies ran while one was open for 2% of the time, Pallas kernels for 33%

profile of v1, /device:TPU:0, one launch (start us, length us, event | category | flops | bytes accessed | tf_op | source)
XLA Modules:
  0.0 273.4 jit_solution(6868463120703001537)
XLA Ops:
  7.9 4.2 %pack.1.refs_2_ = bf16[4,3,128,1024]{3,2,1,0:T(8,128)(2,1)} custom-call(bf16[128,4096]{1,0:T(8,128)(2,1)} %refs_0_.2, bf16[128,4096]{1,0:T(8,128)(2,1)} %refs_1_.2, bf16[128,4096]{1,0:T(8,128)(2,1)} %refs_2_.1), custom_call_target="tpu_custom_call" | custom-call | tf_op jit(solution)/shard_map/pack/pallas_call | solution.py:282
  12.1 4.2 %all-to-all-start = ((bf16[4,3,128,1024]{3,2,1,0:T(8,128)(2,1)}), bf16[4,3,128,1024]{3,2,1,0:T(8,128)(2,1)S(1)}, u32[]{:S(2)}, u32[]{:S(2)}) async-start(bf16[4,3,128,1024]{3,2,1,0:T(8,128)(2,1)} %pack.1.refs_2_), calls=%async_computation | async-start | bytes 6291456 | tf_op jit(solution)/shard_map/all_to_all | solution.py:589
  16.3 3.5 %split.1 = (bf16[128,2048]{1,0:T(8,128)(2,1)}, bf16[128,2048]{1,0:T(8,128)(2,1)}) custom-call(s32[1]{0:T(128)} %bitcast.y_ref, bf16[128,4096]{1,0:T(8,128)(2,1)} %refs_1_.3, bf16[128,4096]{1,0:T(8,128)(2,1)} %refs_1_.3, bf16[4,3,128,1024]{3,2,1,0:T(8,128)(2,1)} %pack.1.refs_2_), custom_call_target="tpu_custom_call" | custom-call | tf_op jit(solution)/shard_map/split/pallas_call | solution.py:354
  19.8 2.5 collective-permute-start
  22.3 12.7 %collective-permute-done = bf16[128,2048]{1,0:T(8,128)(2,1)S(1)} collective-permute-done((bf16[128,2048]{1,0:T(8,128)(2,1)}, bf16[128,2048]{1,0:T(8,128)(2,1)S(1)}, u32[]{:S(2)}, u32[]{:S(2)}) %collective-permute-start) | collective-permute-done | bytes 524320 | tf_op jit(solution)/shard_map/ppermute | solution.py:323
  35.8 3.4 %join.2.refs_1_.refs_0_ = bf16[2,1,128,2048]{3,2,1,0:T(8,128)(2,1)} custom-call(bf16[1,1,128,2048]{3,2,1,0:T(8,128)(2,1)} %bitcast.12, bf16[1,1,128,2048]{3,2,1,0:T(8,128)(2,1)} %bitcast.13), custom_call_target="tpu_custom_call" | custom-call | tf_op jit(solution)/shard_map/join/pallas_call | solution.py:384
  42.3 6.7 %tables.1 = (bf16[8192,256]{1,0:T(8,128)(2,1)}, bf16[8192,256]{1,0:T(8,128)(2,1)}) custom-call(f32[64,256]{1,0:T(8,128)} %pad.8.fwd_ref, f32[64,256]{1,0:T(8,128)} %pad.9.bwd_ref), custom_call_target="tpu_custom_call" | custom-call | tf_op jit(solution)/shard_map/tables/pallas_call | solution.py:41
  49.0 5.2 %all-to-all-done.x_ref.before_ref = bf16[4,3,128,1024]{3,2,1,0:T(8,128)(2,1)S(1)} async-done(((bf16[4,3,128,1024]{3,2,1,0:T(8,128)(2,1)}), bf16[4,3,128,1024]{3,2,1,0:T(8,128)(2,1)S(1)}, u32[]{:S(2)}, u32[]{:S(2)}) %all-to-all-start) | async-done | bytes 3145760 | tf_op jit(solution)/shard_map/all_to_all | solution.py:589
  58.1 3.9 %collective-permute-start.2 = (bf16[176,1024]{1,0:T(8,128)(2,1)}, bf16[176,1024]{1,0:T(8,128)(2,1)S(1)}, u32[]{:S(2)}, u32[]{:S(2)}) collective-permute-start(bf16[176,1024]{1,0:T(8,128)(2,1)} %tail.1), channel_id=1, source_target_pairs={{0,4},{4,8},{8,12},{12,16},{16,20},{20,24},{24,28},{1,5},{5,9},{9,... | collective-permute-start | bytes 1081352 | tf_op jit(solution)/shard_map/ppermute | solution.py:318
  62.0 13.9 %collective-permute-done.1.refs_1_ = bf16[2,1,128,2048]{3,2,1,0:T(8,128)(2,1)} collective-permute-done((bf16[2,1,128,2048]{3,2,1,0:T(8,128)(2,1)}, bf16[2,1,128,2048]{3,2,1,0:T(8,128)(2,1)}, u32[]{:S(2)}, u32[]{:S(2)}) %collective-permute-start.1) | collective-permute-done | bytes 1048608 | tf_op jit(solution)/shard_map/ppermute | solution.py:327
  76.6 3.8 %join.3._.a_ref = bf16[2,2,128,2048]{3,2,1,0:T(8,128)(2,1)} custom-call(bf16[2,1,128,2048]{3,2,1,0:T(8,128)(2,1)} %join.2.refs_1_.refs_0_, bf16[2,1,128,2048]{3,2,1,0:T(8,128)(2,1)} %collective-permute-done.1.refs_1_, bf16[176,1024]{1,0:T(8,128)(2,1)} %copy-done.4), custom_call_target="tpu_custom_call" | custom-call | tf_op jit(solution)/shard_map/join/pallas_call | solution.py:384
  80.9 7.4 %forward.2 = (bf16[512,512]{1,0:T(8,128)(2,1)}, f32[3,512,512]{2,1,0:T(8,128)}, f32[512,512]{1,0:T(8,128)}) custom-call(s32[4]{0:T(128)} %shift-left_add_fusion.place_ref, bf16[4,3,128,1024]{3,2,1,0:T(8,128)(2,1)} %copy-done, bf16[176,1024]{1,0:T(8,128)(2,1)} %copy-done.4, f32[3,7,1024]{2,1,0:T(8,128)} %taps_ref.9, f32[1,1024]{1,0:T(1,128)} %bitcast.18, ...), custom_call_target="tpu_custom_call" | custom-call | tf_op jit(solution)/shard_map/forward/pallas_call | solution.py:111
  88.3 3.8 %collective-permute-start.4 = (bf16[512,512]{1,0:T(8,128)(2,1)}, bf16[512,512]{1,0:T(8,128)(2,1)S(1)}, u32[]{:S(2)}, u32[]{:S(2)}) collective-permute-start(bf16[512,512]{1,0:T(8,128)(2,1)} %get-tuple-element.35._.refs_0_), channel_id=1, source_target_pairs={{0,4},{4,0},{1,5},{5,1},{2,6},{6,2},{3,7},{7,3},{8,12},{12,8},{9,1... | collective-permute-start | bytes 1572872 | tf_op jit(solution)/shard_map/ppermute | solution.py:323
  92.1 7.4 %forward.3 = (bf16[512,512]{1,0:T(8,128)(2,1)}, f32[3,512,512]{2,1,0:T(8,128)}, f32[512,512]{1,0:T(8,128)}) custom-call(s32[4]{0:T(128)} %shift-left_add_fusion.place_ref, bf16[4,3,128,1024]{3,2,1,0:T(8,128)(2,1)} %copy-done, bf16[176,1024]{1,0:T(8,128)(2,1)} %copy-done.4, f32[3,7,1024]{2,1,0:T(8,128)} %taps_ref.9, f32[1,1024]{1,0:T(1,128)} %bitcast.19, ...), custom_call_target="tpu_custom_call" | custom-call | tf_op jit(solution)/shard_map/forward/pallas_call | solution.py:111
  100.9 7.1 %mixed_grad.2 = (bf16[512,1024]{1,0:T(8,128)(2,1)}, bf16[144,1024]{1,0:T(8,128)(2,1)}) custom-call(s32[4]{0:T(128)} %shift-left_add_fusion.place_ref, bf16[2,2,128,2048]{3,2,1,0:T(8,128)(2,1)} %join.3._.a_ref, bf16[2,2,128,2048]{3,2,1,0:T(8,128)(2,1)} %copy-done.1, bf16[1024,2048]{1,0:T(8,128)(2,1)} %all-gather.2.cloned.1.call-done.w_ref, ...), custom_call_target="tpu_custom_call" | custom-call | tf_op jit(solution)/shard_map/mixed_grad/pallas_call | solution.py:428
  108.8 7.4 %mixed_grad.3 = (f32[512,1024]{1,0:T(8,128)}, f32[144,1024]{1,0:T(8,128)}) custom-call(s32[4]{0:T(128)} %shift-left_add_fusion.place_ref, bf16[2,2,128,2048]{3,2,1,0:T(8,128)(2,1)} %join.3._.a_ref, bf16[2,2,128,2048]{3,2,1,0:T(8,128)(2,1)} %copy-done.1, bf16[1024,2048]{1,0:T(8,128)(2,1)} %all-gather.2.cloned.1.call-done.w_ref, ...), custom_call_target="tpu_custom_call" | custom-call | tf_op jit(solution)/shard_map/mixed_grad/pallas_call | solution.py:428
  118.0 2.8 %head.1 = (bf16[192,1024]{1,0:T(8,128)(2,1)}, bf16[512,1024]{1,0:T(8,128)(2,1)}) custom-call(f32[144,1024]{1,0:T(8,128)} %get-tuple-element.39.mo_ref, bf16[144,1024]{1,0:T(8,128)(2,1)} %copy-done.10, f32[3,512,512]{2,1,0:T(8,128)} %get-tuple-element.41.refs_0_.f_ref, ...), custom_call_target="tpu_custom_call", output_to_operand_aliasing={{1}: (6, {})} | custom-call | tf_op jit(solution)/shard_map/head/pallas_call | solution.py:549
  124.1 6.0 %weight_grad.2.refs_3_ = bf16[1024,2048]{1,0:T(8,128)(2,1)} custom-call(bf16[2,2,128,2048]{3,2,1,0:T(8,128)(2,1)} %join.3._.a_ref, bf16[2,2,128,2048]{3,2,1,0:T(8,128)(2,1)} %copy-done.1, bf16[512,512]{1,0:T(8,128)(2,1)} %get-tuple-element.35._.refs_0_, bf16[512,512]{1,0:T(8,128)(2,1)} %copy-done.5, bf16[192,1024]{1,0:T(8,128)(2,1)} %get-tuple-element.46.refs_2_), custom_call_target="tpu_custom_call" | custom-call | tf_op jit(solution)/shard_map/weight_grad/pallas_call | solution.py:473
  130.2 33.9 %collective-permute-done.8.refs_1_ = bf16[512,512]{1,0:T(8,128)(2,1)S(1)} collective-permute-done((bf16[512,512]{1,0:T(8,128)(2,1)S(1)}, bf16[512,512]{1,0:T(8,128)(2,1)S(1)}, u32[]{:S(2)}, u32[]{:S(2)}) %collective-permute-start.8) | collective-permute-done | bytes 524320 | tf_op jit(solution)/shard_map/ppermute | solution.py:323
  165.9 6.0 %weight_grad.3 = bf16[1024,2048]{1,0:T(8,128)(2,1)} custom-call(bf16[2,2,128,2048]{3,2,1,0:T(8,128)(2,1)} %join.3._.a_ref, bf16[2,2,128,2048]{3,2,1,0:T(8,128)(2,1)} %copy-done.1, bf16[512,512]{1,0:T(8,128)(2,1)} %get-tuple-element.36.refs_0_, bf16[512,512]{1,0:T(8,128)(2,1)} %copy-done.8, ...), custom_call_target="tpu_custom_call", output_to_operand_aliasing={{}: (5, {})} | custom-call | tf_op jit(solution)/shard_map/weight_grad/pallas_call | solution.py:473
  172.9 10.6 %backward.3 = (bf16[4,3,128,512]{3,2,1,0:T(8,128)(2,1)}, f32[3,8,512]{2,1,0:T(8,128)}, f32[32,128]{1,0:T(8,128)}) custom-call(f32[512,1024]{1,0:T(8,128)} %get-tuple-element.38.mo_ref, bf16[512,1024]{1,0:T(8,128)(2,1)} %copy-done.15, f32[3,512,512]{2,1,0:T(8,128)} %get-tuple-element.43.refs_2_.f_ref, f32[512,512]{1,0:T(8,128)} %get-tuple-element.44.refs_3_.filt_ref, ...), custom_call_target="tpu_custom_call" | custom-call | flops 99999997952 | bytes 9437184 | tf_op jit(solution)/shard_map/backward/pallas_call | solution.py:236
  183.5 3.6 %all-to-all-start.2 = ((bf16[4,3,128,512]{3,2,1,0:T(8,128)(2,1)}), bf16[4,3,128,512]{3,2,1,0:T(8,128)(2,1)S(1)}, u32[]{:S(2)}, u32[]{:S(2)}) async-start(bf16[4,3,128,512]{3,2,1,0:T(8,128)(2,1)} %get-tuple-element.49), calls=%async_computation.2 | async-start | bytes 3145728 | tf_op jit(solution)/shard_map/all_to_all | solution.py:627
  187.1 10.8 %backward.2 = (bf16[4,3,128,512]{3,2,1,0:T(8,128)(2,1)}, f32[3,8,512]{2,1,0:T(8,128)}, f32[32,128]{1,0:T(8,128)}) custom-call(f32[512,1024]{1,0:T(8,128)} %get-tuple-element.38.mo_ref, bf16[512,1024]{1,0:T(8,128)(2,1)} %copy-done.15, f32[3,512,512]{2,1,0:T(8,128)} %get-tuple-element.41.refs_0_.f_ref, f32[512,512]{1,0:T(8,128)} %get-tuple-element.42.refs_1_.filt_ref, ...), custom_call_target="tpu_custom_call" | custom-call | flops 99999997952 | bytes 9437184 | tf_op jit(solution)/shard_map/backward/pallas_call | solution.py:236
  199.5 7.6 %all-to-all-done.2.refs_1_ = bf16[4,3,128,512]{3,2,1,0:T(8,128)(2,1)S(1)} async-done(((bf16[4,3,128,512]{3,2,1,0:T(8,128)(2,1)}), bf16[4,3,128,512]{3,2,1,0:T(8,128)(2,1)S(1)}, u32[]{:S(2)}, u32[]{:S(2)}) %all-to-all-start.2) | async-done | bytes 1572896 | tf_op jit(solution)/shard_map/all_to_all | solution.py:627
  207.2 3.6 %all-to-all-start.1 = ((bf16[4,3,128,512]{3,2,1,0:T(8,128)(2,1)}), bf16[4,3,128,512]{3,2,1,0:T(8,128)(2,1)S(1)}, u32[]{:S(2)}, u32[]{:S(2)}) async-start(bf16[4,3,128,512]{3,2,1,0:T(8,128)(2,1)} %get-tuple-element.48), calls=%async_computation.1 | async-start | bytes 3145728 | tf_op jit(solution)/shard_map/all_to_all | solution.py:627
  213.0 4.1 %collective-permute-done.9 = f32[32,1024]{1,0:T(8,128)S(1)} collective-permute-done((f32[32,1024]{1,0:T(8,128)S(1)}, f32[32,1024]{1,0:T(8,128)S(1)}, u32[]{:S(2)}, u32[]{:S(2)}) %collective-permute-start.9) | collective-permute-done | bytes 131104 | tf_op jit(solution)/shard_map/ppermute | solution.py:327
  217.1 9.1 %collective-permute-start.10 = (f32[32,1024]{1,0:T(8,128)S(1)}, f32[32,1024]{1,0:T(8,128)S(1)}, u32[]{:S(2)}, u32[]{:S(2)}) collective-permute-start(f32[32,1024]{1,0:T(8,128)S(1)} %fusion), channel_id=1, source_target_pairs={{0,8},{8,0},{16,24},{24,16},{1,9},{9,1},{17,25},{25,17},{2,10},{10... | collective-permute-start | bytes 393224 | tf_op jit(solution)/shard_map/ppermute | solution.py:327
  226.2 10.4 %collective-permute-done.10 = f32[32,1024]{1,0:T(8,128)S(1)} collective-permute-done((f32[32,1024]{1,0:T(8,128)S(1)}, f32[32,1024]{1,0:T(8,128)S(1)}, u32[]{:S(2)}, u32[]{:S(2)}) %collective-permute-start.10) | collective-permute-done | bytes 131104 | tf_op jit(solution)/shard_map/ppermute | solution.py:327
  236.7 3.7 %collective-permute-start.11 = (f32[32,1024]{1,0:T(8,128)S(1)}, f32[32,1024]{1,0:T(8,128)S(1)}, u32[]{:S(2)}, u32[]{:S(2)}) collective-permute-start(f32[32,1024]{1,0:T(8,128)S(1)} %add.20), channel_id=1, source_target_pairs={{0,16},{8,24},{16,0},{24,8},{1,17},{9,25},{17,1},{25,9},{2,18},{10... | collective-permute-start | bytes 393224 | tf_op jit(solution)/shard_map/ppermute | solution.py:327
  240.4 15.9 %collective-permute-done.11 = f32[32,1024]{1,0:T(8,128)S(1)} collective-permute-done((f32[32,1024]{1,0:T(8,128)S(1)}, f32[32,1024]{1,0:T(8,128)S(1)}, u32[]{:S(2)}, u32[]{:S(2)}) %collective-permute-start.11) | collective-permute-done | bytes 131104 | tf_op jit(solution)/shard_map/ppermute | solution.py:327
  258.7 4.2 %unpack.1 = (bf16[128,4096]{1,0:T(8,128)(2,1)}, bf16[128,4096]{1,0:T(8,128)(2,1)}, bf16[128,4096]{1,0:T(8,128)(2,1)}) custom-call(bf16[4,3,128,512]{3,2,1,0:T(8,128)(2,1)} %copy-done.3, bf16[4,3,128,512]{3,2,1,0:T(8,128)(2,1)} %copy-done.2), custom_call_target="tpu_custom_call" | custom-call | tf_op jit(solution)/shard_map/unpack/pallas_call | solution.py:305
  263.7 2.8 %convert_element_type.7 = f32[1024,512]{1,0:T(8,128)} convert(bf16[1024,512]{1,0:T(8,128)(2,1)} %reduce-scatter.2.cloned.1.call-done) | non-fusion elementwise | flops 524288 | bytes 3145728 | tf_op jit(solution)/shard_map/convert_element_type | solution.py:646
  (68 shorter events, 27.1 us)
Async XLA Ops:
  7.2 92.4 %all-gather.2.cloned.1.call-start = ((), (), s32[]{:S(2)}) async-start(), calls=%async_computation.4 | async-start | bytes 5242880 | tf_op jit(solution)/shard_map/all_gather | solution.py:584
  12.1 42.0 %all-to-all-start = ((bf16[4,3,128,1024]{3,2,1,0:T(8,128)(2,1)}), bf16[4,3,128,1024]{3,2,1,0:T(8,128)(2,1)S(1)}, u32[]{:S(2)}, u32[]{:S(2)}) async-start(bf16[4,3,128,1024]{3,2,1,0:T(8,128)(2,1)} %pack.1.refs_2_), calls=%async_computation | async-start | bytes 6291456 | tf_op jit(solution)/shard_map/all_to_all | solution.py:589
  16.3 247.4 %reduce-scatter.2.cloned.1.call-start = ((), (), s32[]{:S(2)}) async-start(), calls=%async_computation.5 | async-start | bytes 5242880 | tf_op jit(solution)/shard_map/reduce_scatter | solution.py:619
  16.3 24.6 %copy-start.11 = (f32[128,64]{0,1:T(8,128)S(1)}, f32[128,64]{0,1:T(8,128)}, u32[]{:S(2)}) copy-start(f32[128,64]{0,1:T(8,128)} %param.14) | copy-start | bytes 98308
  19.8 15.2 %collective-permute-start = (bf16[128,2048]{1,0:T(8,128)(2,1)}, bf16[128,2048]{1,0:T(8,128)(2,1)S(1)}, u32[]{:S(2)}, u32[]{:S(2)}) collective-permute-start(bf16[128,2048]{1,0:T(8,128)(2,1)} %get-tuple-element.33), channel_id=1, source_target_pairs={{0,4},{4,0},{1,5},{5,1},{2,6},{6,2},{3,7},{7,3},{8,12},{12,8},{9,1... | collective-permute-start | bytes 1572872 | tf_op jit(solution)/shard_map/ppermute | solution.py:323
  35.0 0.8 copy-start.7
  39.2 36.7 %collective-permute-start.1 = (bf16[2,1,128,2048]{3,2,1,0:T(8,128)(2,1)}, bf16[2,1,128,2048]{3,2,1,0:T(8,128)(2,1)}, u32[]{:S(2)}, u32[]{:S(2)}) collective-permute-start(bf16[2,1,128,2048]{3,2,1,0:T(8,128)(2,1)} %join.2.refs_1_.refs_0_), channel_id=1, source_target_pairs={{0,2},{1,3},{2,0},{3,1},{4,6},{5,7},{6,4},{7,5},{8,10},{9,11},{10,... | collective-permute-start | bytes 3145736 | tf_op jit(solution)/shard_map/ppermute | solution.py:327
  54.1 1.6 copy-start
  58.1 17.8 %collective-permute-start.2 = (bf16[176,1024]{1,0:T(8,128)(2,1)}, bf16[176,1024]{1,0:T(8,128)(2,1)S(1)}, u32[]{:S(2)}, u32[]{:S(2)}) collective-permute-start(bf16[176,1024]{1,0:T(8,128)(2,1)} %tail.1), channel_id=1, source_target_pairs={{0,4},{4,8},{8,12},{12,16},{16,20},{20,24},{24,28},{1,5},{5,9},{9,... | collective-permute-start | bytes 1081352 | tf_op jit(solution)/shard_map/ppermute | solution.py:318
  75.9 0.7 copy-start.4
  80.4 19.1 %collective-permute-start.3 = (bf16[2,2,128,2048]{3,2,1,0:T(8,128)(2,1)}, bf16[2,2,128,2048]{3,2,1,0:T(8,128)(2,1)S(1)}, u32[]{:S(2)}, u32[]{:S(2)}) collective-permute-start(bf16[2,2,128,2048]{3,2,1,0:T(8,128)(2,1)} %join.3._.a_ref), channel_id=1, source_target_pairs={{0,1},{1,0},{2,3},{3,2},{4,5},{5,4},{6,7},{7,6},{8,9},{9,8},{10,11... | collective-permute-start | bytes 6291464 | tf_op jit(solution)/shard_map/ppermute | solution.py:327
  88.3 19.7 %collective-permute-start.4 = (bf16[512,512]{1,0:T(8,128)(2,1)}, bf16[512,512]{1,0:T(8,128)(2,1)S(1)}, u32[]{:S(2)}, u32[]{:S(2)}) collective-permute-start(bf16[512,512]{1,0:T(8,128)(2,1)} %get-tuple-element.35._.refs_0_), channel_id=1, source_target_pairs={{0,4},{4,0},{1,5},{5,1},{2,6},{6,2},{3,7},{7,3},{8,12},{12,8},{9,1... | collective-permute-start | bytes 1572872 | tf_op jit(solution)/shard_map/ppermute | solution.py:323
  99.5 1.4 copy-start.1
  108.0 9.3 %collective-permute-start.5 = (bf16[144,1024]{1,0:T(8,128)(2,1)}, bf16[144,1024]{1,0:T(8,128)(2,1)S(1)}, u32[]{:S(2)}, u32[]{:S(2)}) collective-permute-start(bf16[144,1024]{1,0:T(8,128)(2,1)} %get-tuple-element.40), channel_id=1, source_target_pairs={{0,4},{4,0},{1,5},{5,1},{2,6},{6,2},{3,7},{7,3},{8,12},{12,8},{9,1... | collective-permute-start | bytes 884744 | tf_op jit(solution)/shard_map/ppermute | solution.py:323
  108.0 0.8 copy-start.5
  118.0 3.6 %copy-start.6 = (bf16[512,512]{1,0:T(8,128)(2,1)S(1)}, bf16[512,512]{1,0:T(8,128)(2,1)}, u32[]{:S(2)}) copy-start(bf16[512,512]{1,0:T(8,128)(2,1)} %get-tuple-element.36.refs_0_) | copy-start | bytes 1572868
  120.8 51.1 %collective-permute-start.6 = (bf16[512,1024]{1,0:T(8,128)(2,1)}, bf16[512,1024]{1,0:T(8,128)(2,1)S(1)}, u32[]{:S(2)}, u32[]{:S(2)}) collective-permute-start(bf16[512,1024]{1,0:T(8,128)(2,1)} %get-tuple-element.45), channel_id=1, source_target_pairs={{0,4},{4,0},{1,5},{5,1},{2,6},{6,2},{3,7},{7,3},{8,12},{12,8},{9,1... | collective-permute-start | bytes 3145736 | tf_op jit(solution)/shard_map/ppermute | solution.py:323
  121.7 42.4 %collective-permute-start.8 = (bf16[512,512]{1,0:T(8,128)(2,1)S(1)}, bf16[512,512]{1,0:T(8,128)(2,1)S(1)}, u32[]{:S(2)}, u32[]{:S(2)}) collective-permute-start(bf16[512,512]{1,0:T(8,128)(2,1)S(1)} %copy-done.6), channel_id=1, source_target_pairs={{0,4},{4,0},{1,5},{5,1},{2,6},{6,2},{3,7},{7,3},{8,12},{12,8},{9,1... | collective-permute-start | bytes 1572872 | tf_op jit(solution)/shard_map/ppermute | solution.py:323
  122.9 42.3 %collective-permute-start.7 = (bf16[192,1024]{1,0:T(8,128)(2,1)}, bf16[192,1024]{1,0:T(8,128)(2,1)S(1)}, u32[]{:S(2)}, u32[]{:S(2)}) collective-permute-start(bf16[192,1024]{1,0:T(8,128)(2,1)} %get-tuple-element.46.refs_2_), channel_id=1, source_target_pairs={{4,0},{8,4},{12,8},{16,12},{20,16},{24,20},{28,24},{5,1},{9,5},{13... | collective-permute-start | bytes 1179656 | tf_op jit(solution)/shard_map/ppermute | solution.py:318
  164.1 1.1 copy-start.8
  165.2 0.8 copy-start.9
  172.0 1.0 copy-start.15
  183.5 23.6 %all-to-all-start.2 = ((bf16[4,3,128,512]{3,2,1,0:T(8,128)(2,1)}), bf16[4,3,128,512]{3,2,1,0:T(8,128)(2,1)S(1)}, u32[]{:S(2)}, u32[]{:S(2)}) async-start(bf16[4,3,128,512]{3,2,1,0:T(8,128)(2,1)} %get-tuple-element.49), calls=%async_computation.2 | async-start | bytes 3145728 | tf_op jit(solution)/shard_map/all_to_all | solution.py:627
  187.1 10.9 %copy-start.14 = (f32[32,128]{1,0:T(8,128)S(1)}, f32[32,128]{1,0:T(8,128)}, u32[]{:S(2)}) copy-start(f32[32,128]{1,0:T(8,128)} %get-tuple-element.56) | copy-start | bytes 49156
  187.1 11.6 %copy-start.13 = (f32[3,8,512]{2,1,0:T(8,128)S(1)}, f32[3,8,512]{2,1,0:T(8,128)}, u32[]{:S(2)}) copy-start(f32[3,8,512]{2,1,0:T(8,128)} %get-tuple-element.54) | copy-start | bytes 147460
  207.2 50.4 %copy-start.2 = (bf16[4,3,128,512]{3,2,1,0:T(8,128)(2,1)}, bf16[4,3,128,512]{3,2,1,0:T(8,128)(2,1)S(1)}, u32[]{:S(2)}) copy-start(bf16[4,3,128,512]{3,2,1,0:T(8,128)(2,1)S(1)} %all-to-all-done.2.refs_1_) | copy-start | bytes 4718596
  207.2 50.4 %all-to-all-start.1 = ((bf16[4,3,128,512]{3,2,1,0:T(8,128)(2,1)}), bf16[4,3,128,512]{3,2,1,0:T(8,128)(2,1)S(1)}, u32[]{:S(2)}, u32[]{:S(2)}) async-start(bf16[4,3,128,512]{3,2,1,0:T(8,128)(2,1)} %get-tuple-element.48), calls=%async_computation.1 | async-start | bytes 3145728 | tf_op jit(solution)/shard_map/all_to_all | solution.py:627
  210.7 6.4 %collective-permute-start.9 = (f32[32,1024]{1,0:T(8,128)S(1)}, f32[32,1024]{1,0:T(8,128)S(1)}, u32[]{:S(2)}, u32[]{:S(2)}) collective-permute-start(f32[32,1024]{1,0:T(8,128)S(1)} %pad_maximum_fusion), channel_id=1, source_target_pairs={{0,4},{4,0},{1,5},{5,1},{2,6},{6,2},{3,7},{7,3},{8,12},{12,8},{9,1... | collective-permute-start | bytes 393224 | tf_op jit(solution)/shard_map/ppermute | solution.py:327
  217.1 19.5 %collective-permute-start.10 = (f32[32,1024]{1,0:T(8,128)S(1)}, f32[32,1024]{1,0:T(8,128)S(1)}, u32[]{:S(2)}, u32[]{:S(2)}) collective-permute-start(f32[32,1024]{1,0:T(8,128)S(1)} %fusion), channel_id=1, source_target_pairs={{0,8},{8,0},{16,24},{24,16},{1,9},{9,1},{17,25},{25,17},{2,10},{10... | collective-permute-start | bytes 393224 | tf_op jit(solution)/shard_map/ppermute | solution.py:327
  236.7 19.6 %collective-permute-start.11 = (f32[32,1024]{1,0:T(8,128)S(1)}, f32[32,1024]{1,0:T(8,128)S(1)}, u32[]{:S(2)}, u32[]{:S(2)}) collective-permute-start(f32[32,1024]{1,0:T(8,128)S(1)} %add.20), channel_id=1, source_target_pairs={{0,16},{8,24},{16,0},{24,8},{1,17},{9,25},{17,1},{25,9},{2,18},{10... | collective-permute-start | bytes 393224 | tf_op jit(solution)/shard_map/ppermute | solution.py:327
  256.3 10.2 %copy-start.12 = (f32[3,8,1024]{2,1,0:T(8,128)}, f32[3,8,1024]{2,1,0:T(8,128)S(1)}, u32[]{:S(2)}) copy-start(f32[3,8,1024]{2,1,0:T(8,128)S(1)} %slice_bitcast_fusion) | copy-start | bytes 294916
  257.6 1.1 copy-start.3
  (1 other events, 0.7 us)
Sparse Core Ops, SparseCore 0:
  9.6 83.4 all-gather.1
  172.1 91.5 reduce-scatter.1

commit v2 on v1

--- a/solution.py
+++ b/solution.py
@@ -602,10 +602,12 @@
 
     parts, heads = [], []
     for step in range(1, ys):
-        part, head = mixed_grad(cots, weights, place, step, BF16, [parts[-1] if parts else mixers[-1][0]])
+        part, head = mixed_grad(
+            cots, weights, place, step, BF16, [parts[-1] if parts else mixers[-1][0], *mixed_all[0][1:]]
+        )
         parts.append(part)
         heads.append(around(head, "y", -step))
-    mixed_own, own_head = mixed_grad(cots, weights, place, 0, F32, [parts[-1], *mixed_all[0][1:]])
+    mixed_own, own_head = mixed_grad(cots, weights, place, 0, F32, [parts[-1], *mixed_all[-1][1:]])
     head_rest = heads[0] if len(heads) == 1 else sum(piece.astype(F32) for piece in heads)
     head, parts[-1] = head_of(own_head, head_rest, mixers, parts[-1])
     rest = [around(parts[step - 1], "y", -step) for step in range(1, ys)]

time: 275 us -> 272 us (0.989)
    ppermute x5, waiting for transfers between devices: 47.8 us -> 18.8 us  [around(): lax.ppermute(block, axis, [(i, (i + distance) % size) for i in range(size)])]
    ppermute x2, waiting for transfers between devices: 1.09 us -> 24.6 us  [along(): lax.ppermute(block, axis, [(i, i + distance) for i in range(size) if 0 <=...]
    unnamed x32 -> x30, local copies, waits for them, and re-layouts: 8.93 us -> 9.12 us
  transfers between devices with their start and end apart: 17 -> 17, of which waited for: 11 -> 11; matrix products, arithmetic and copies ran while one was open for 2% -> 2% of each run, Pallas kernels for 33% -> 34%
where the time goes in v2:
time: 272 us; the launch traced here: 270 us
  waiting for transfers between devices  105 us (39%)
  Pallas kernels  93.4 us (34%)
  starting transfers between devices  40.8 us (15%)
  between operations  14.2 us (5%)
  local copies, waits for them, and re-layouts  11.8 us (4%)
  other arithmetic  4.95 us (2%)
    ppermute x5, waiting for transfers between devices, across(): lax.ppermute(block, axis, [(i, i ^ bit) for i in range(lax.axis_size(axis...  47.1 us
    ppermute x2, waiting for transfers between devices, along(): lax.ppermute(block, axis, [(i, i + distance) for i in range(size) if 0 <=...  24.6 us
    pallas_call x2, Pallas kernels, backward(): pl.pallas_call(backward_kernel, grid=(tiles,), in_specs=[tok, tok, pl.Blo...  21.5 us
    ppermute x5, waiting for transfers between devices, around(): lax.ppermute(block, axis, [(i, (i + distance) % size) for i in range(size)])  18.8 us
    pallas_call x2, Pallas kernels, forward(): pl.pallas_call(forward_kernel, grid_spec=pltpu.PrefetchScalarGridSpec(num...  14.8 us
    pallas_call x2, Pallas kernels, mixed_grad(): pl.pallas_call(functools.partial(mixed_grad_kernel, len(after)), grid_spe...  14.4 us
    ppermute x5, starting transfers between devices, across(): lax.ppermute(block, axis, [(i, i ^ bit) for i in range(lax.axis_size(axis...  14.1 us
    pallas_call x2, Pallas kernels, weight_grad(): pl.pallas_call(functools.partial(weight_grad_kernel, scale), grid=(Z,), i...  12.1 us
  transfers between devices with their start and end apart: 17, of which 11 were waited for; matrix products, arithmetic and copies ran while one was open for 2% of the time, Pallas kernels for 34%

profile of v2, /device:TPU:0, one launch (start us, length us, event | category | flops | bytes accessed | tf_op | source)
XLA Modules:
  0.0 269.9 jit_solution(2188151219209360024)
XLA Ops:
  7.9 4.2 %pack.1.refs_2_ = bf16[4,3,128,1024]{3,2,1,0:T(8,128)(2,1)} custom-call(bf16[128,4096]{1,0:T(8,128)(2,1)} %refs_0_.2, bf16[128,4096]{1,0:T(8,128)(2,1)} %refs_1_.2, bf16[128,4096]{1,0:T(8,128)(2,1)} %refs_2_.1), custom_call_target="tpu_custom_call" | custom-call | tf_op jit(solution)/shard_map/pack/pallas_call | solution.py:282
  12.1 4.2 %all-to-all-start = ((bf16[4,3,128,1024]{3,2,1,0:T(8,128)(2,1)}), bf16[4,3,128,1024]{3,2,1,0:T(8,128)(2,1)S(1)}, u32[]{:S(2)}, u32[]{:S(2)}) async-start(bf16[4,3,128,1024]{3,2,1,0:T(8,128)(2,1)} %pack.1.refs_2_), calls=%async_computation | async-start | bytes 6291456 | tf_op jit(solution)/shard_map/all_to_all | solution.py:589
  16.3 3.5 %split.1 = (bf16[128,2048]{1,0:T(8,128)(2,1)}, bf16[128,2048]{1,0:T(8,128)(2,1)}) custom-call(s32[1]{0:T(128)} %bitcast.y_ref, bf16[128,4096]{1,0:T(8,128)(2,1)} %refs_1_.3, bf16[128,4096]{1,0:T(8,128)(2,1)} %refs_1_.3, bf16[4,3,128,1024]{3,2,1,0:T(8,128)(2,1)} %pack.1.refs_2_), custom_call_target="tpu_custom_call" | custom-call | tf_op jit(solution)/shard_map/split/pallas_call | solution.py:354
  22.3 12.7 %collective-permute-done = bf16[128,2048]{1,0:T(8,128)(2,1)S(1)} collective-permute-done((bf16[128,2048]{1,0:T(8,128)(2,1)}, bf16[128,2048]{1,0:T(8,128)(2,1)S(1)}, u32[]{:S(2)}, u32[]{:S(2)}) %collective-permute-start) | collective-permute-done | bytes 524320 | tf_op jit(solution)/shard_map/ppermute | solution.py:323
  35.8 3.4 %join.2.refs_1_.refs_0_ = bf16[2,1,128,2048]{3,2,1,0:T(8,128)(2,1)} custom-call(bf16[1,1,128,2048]{3,2,1,0:T(8,128)(2,1)} %bitcast.12, bf16[1,1,128,2048]{3,2,1,0:T(8,128)(2,1)} %bitcast.13), custom_call_target="tpu_custom_call" | custom-call | tf_op jit(solution)/shard_map/join/pallas_call | solution.py:384
  42.3 6.7 %tables.1 = (bf16[8192,256]{1,0:T(8,128)(2,1)}, bf16[8192,256]{1,0:T(8,128)(2,1)}) custom-call(f32[64,256]{1,0:T(8,128)} %pad.8.fwd_ref, f32[64,256]{1,0:T(8,128)} %pad.9.bwd_ref), custom_call_target="tpu_custom_call" | custom-call | tf_op jit(solution)/shard_map/tables/pallas_call | solution.py:41
  49.0 5.2 %all-to-all-done.x_ref.before_ref = bf16[4,3,128,1024]{3,2,1,0:T(8,128)(2,1)S(1)} async-done(((bf16[4,3,128,1024]{3,2,1,0:T(8,128)(2,1)}), bf16[4,3,128,1024]{3,2,1,0:T(8,128)(2,1)S(1)}, u32[]{:S(2)}, u32[]{:S(2)}) %all-to-all-start) | async-done | bytes 3145760 | tf_op jit(solution)/shard_map/all_to_all | solution.py:589
  58.1 3.9 %collective-permute-start.2 = (bf16[176,1024]{1,0:T(8,128)(2,1)}, bf16[176,1024]{1,0:T(8,128)(2,1)S(1)}, u32[]{:S(2)}, u32[]{:S(2)}) collective-permute-start(bf16[176,1024]{1,0:T(8,128)(2,1)} %tail.1), channel_id=1, source_target_pairs={{0,4},{4,8},{8,12},{12,16},{16,20},{20,24},{24,28},{1,5},{5,9},{9,... | collective-permute-start | bytes 1081352 | tf_op jit(solution)/shard_map/ppermute | solution.py:318
  62.0 13.9 %collective-permute-done.1.refs_1_ = bf16[2,1,128,2048]{3,2,1,0:T(8,128)(2,1)} collective-permute-done((bf16[2,1,128,2048]{3,2,1,0:T(8,128)(2,1)}, bf16[2,1,128,2048]{3,2,1,0:T(8,128)(2,1)}, u32[]{:S(2)}, u32[]{:S(2)}) %collective-permute-start.1) | collective-permute-done | bytes 1048608 | tf_op jit(solution)/shard_map/ppermute | solution.py:327
  76.6 3.8 %join.3._.a_ref = bf16[2,2,128,2048]{3,2,1,0:T(8,128)(2,1)} custom-call(bf16[2,1,128,2048]{3,2,1,0:T(8,128)(2,1)} %join.2.refs_1_.refs_0_, bf16[2,1,128,2048]{3,2,1,0:T(8,128)(2,1)} %collective-permute-done.1.refs_1_, bf16[176,1024]{1,0:T(8,128)(2,1)} %copy-done.4), custom_call_target="tpu_custom_call" | custom-call | tf_op jit(solution)/shard_map/join/pallas_call | solution.py:384
  80.9 7.4 %forward.2 = (bf16[512,512]{1,0:T(8,128)(2,1)}, f32[3,512,512]{2,1,0:T(8,128)}, f32[512,512]{1,0:T(8,128)}) custom-call(s32[4]{0:T(128)} %shift-left_add_fusion.place_ref, bf16[4,3,128,1024]{3,2,1,0:T(8,128)(2,1)} %copy-done, bf16[176,1024]{1,0:T(8,128)(2,1)} %copy-done.4, f32[3,7,1024]{2,1,0:T(8,128)} %taps_ref.9, f32[1,1024]{1,0:T(1,128)} %bitcast.18, ...), custom_call_target="tpu_custom_call" | custom-call | tf_op jit(solution)/shard_map/forward/pallas_call | solution.py:111
  88.3 3.8 %collective-permute-start.4 = (bf16[512,512]{1,0:T(8,128)(2,1)}, bf16[512,512]{1,0:T(8,128)(2,1)S(1)}, u32[]{:S(2)}, u32[]{:S(2)}) collective-permute-start(bf16[512,512]{1,0:T(8,128)(2,1)} %get-tuple-element.35._.refs_0_), channel_id=1, source_target_pairs={{0,4},{4,0},{1,5},{5,1},{2,6},{6,2},{3,7},{7,3},{8,12},{12,8},{9,1... | collective-permute-start | bytes 1572872 | tf_op jit(solution)/shard_map/ppermute | solution.py:323
  92.2 7.4 %forward.3 = (bf16[512,512]{1,0:T(8,128)(2,1)}, f32[3,512,512]{2,1,0:T(8,128)}, f32[512,512]{1,0:T(8,128)}) custom-call(s32[4]{0:T(128)} %shift-left_add_fusion.place_ref, bf16[4,3,128,1024]{3,2,1,0:T(8,128)(2,1)} %copy-done, bf16[176,1024]{1,0:T(8,128)(2,1)} %copy-done.4, f32[3,7,1024]{2,1,0:T(8,128)} %taps_ref.9, f32[1,1024]{1,0:T(1,128)} %bitcast.19, ...), custom_call_target="tpu_custom_call" | custom-call | tf_op jit(solution)/shard_map/forward/pallas_call | solution.py:111
  99.6 5.6 %collective-permute-done.4.refs_1_ = bf16[512,512]{1,0:T(8,128)(2,1)S(1)} collective-permute-done((bf16[512,512]{1,0:T(8,128)(2,1)}, bf16[512,512]{1,0:T(8,128)(2,1)S(1)}, u32[]{:S(2)}, u32[]{:S(2)}) %collective-permute-start.4) | collective-permute-done | bytes 524320 | tf_op jit(solution)/shard_map/ppermute | solution.py:323
  106.7 7.1 %mixed_grad.2 = (bf16[512,1024]{1,0:T(8,128)(2,1)}, bf16[144,1024]{1,0:T(8,128)(2,1)}) custom-call(s32[4]{0:T(128)} %shift-left_add_fusion.place_ref, bf16[2,2,128,2048]{3,2,1,0:T(8,128)(2,1)} %join.3._.a_ref, bf16[2,2,128,2048]{3,2,1,0:T(8,128)(2,1)} %copy-done.1, bf16[1024,2048]{1,0:T(8,128)(2,1)} %all-gather.2.cloned.1.call-done.w_ref, ...), custom_call_target="tpu_custom_call" | custom-call | tf_op jit(solution)/shard_map/mixed_grad/pallas_call | solution.py:428
  117.0 7.3 %mixed_grad.3 = (f32[512,1024]{1,0:T(8,128)}, f32[144,1024]{1,0:T(8,128)}) custom-call(s32[4]{0:T(128)} %shift-left_add_fusion.place_ref, bf16[2,2,128,2048]{3,2,1,0:T(8,128)(2,1)} %join.3._.a_ref, bf16[2,2,128,2048]{3,2,1,0:T(8,128)(2,1)} %copy-done.1, bf16[1024,2048]{1,0:T(8,128)(2,1)} %all-gather.2.cloned.1.call-done.w_ref, ...), custom_call_target="tpu_custom_call" | custom-call | tf_op jit(solution)/shard_map/mixed_grad/pallas_call | solution.py:428
  125.1 2.7 head.1
  130.8 6.0 %weight_grad.2.refs_3_ = bf16[1024,2048]{1,0:T(8,128)(2,1)} custom-call(bf16[2,2,128,2048]{3,2,1,0:T(8,128)(2,1)} %join.3._.a_ref, bf16[2,2,128,2048]{3,2,1,0:T(8,128)(2,1)} %copy-done.1, bf16[512,512]{1,0:T(8,128)(2,1)} %get-tuple-element.35._.refs_0_, bf16[512,512]{1,0:T(8,128)(2,1)} %copy-done.5, bf16[192,1024]{1,0:T(8,128)(2,1)} %get-tuple-element.46.refs_2_), custom_call_target="tpu_custom_call" | custom-call | tf_op jit(solution)/shard_map/weight_grad/pallas_call | solution.py:473
  136.9 24.6 %collective-permute-done.8.n_ref.refs_2_ = bf16[192,1024]{1,0:T(8,128)(2,1)S(1)} collective-permute-done((bf16[192,1024]{1,0:T(8,128)(2,1)}, bf16[192,1024]{1,0:T(8,128)(2,1)S(1)}, u32[]{:S(2)}, u32[]{:S(2)}) %collective-permute-start.8) | collective-permute-done | bytes 393248 | tf_op jit(solution)/shard_map/ppermute | solution.py:318
  162.2 6.1 %weight_grad.3 = bf16[1024,2048]{1,0:T(8,128)(2,1)} custom-call(bf16[2,2,128,2048]{3,2,1,0:T(8,128)(2,1)} %join.3._.a_ref, bf16[2,2,128,2048]{3,2,1,0:T(8,128)(2,1)} %copy-done.1, bf16[512,512]{1,0:T(8,128)(2,1)} %get-tuple-element.36.refs_0_, bf16[512,512]{1,0:T(8,128)(2,1)} %copy-done.6, ...), custom_call_target="tpu_custom_call", output_to_operand_aliasing={{}: (5, {})} | custom-call | tf_op jit(solution)/shard_map/weight_grad/pallas_call | solution.py:473
  169.3 10.6 %backward.3 = (bf16[4,3,128,512]{3,2,1,0:T(8,128)(2,1)}, f32[3,8,512]{2,1,0:T(8,128)}, f32[32,128]{1,0:T(8,128)}) custom-call(f32[512,1024]{1,0:T(8,128)} %get-tuple-element.38.mo_ref, bf16[512,1024]{1,0:T(8,128)(2,1)} %copy-done.14, f32[3,512,512]{2,1,0:T(8,128)} %get-tuple-element.43.refs_2_.f_ref, f32[512,512]{1,0:T(8,128)} %get-tuple-element.44.refs_3_.filt_ref, ...), custom_call_target="tpu_custom_call" | custom-call | flops 99999997952 | bytes 9437184 | tf_op jit(solution)/shard_map/backward/pallas_call | solution.py:236
  179.8 3.6 %all-to-all-start.2 = ((bf16[4,3,128,512]{3,2,1,0:T(8,128)(2,1)}), bf16[4,3,128,512]{3,2,1,0:T(8,128)(2,1)S(1)}, u32[]{:S(2)}, u32[]{:S(2)}) async-start(bf16[4,3,128,512]{3,2,1,0:T(8,128)(2,1)} %get-tuple-element.49), calls=%async_computation.2 | async-start | bytes 3145728 | tf_op jit(solution)/shard_map/all_to_all | solution.py:629
  183.4 10.9 %backward.2 = (bf16[4,3,128,512]{3,2,1,0:T(8,128)(2,1)}, f32[3,8,512]{2,1,0:T(8,128)}, f32[32,128]{1,0:T(8,128)}) custom-call(f32[512,1024]{1,0:T(8,128)} %get-tuple-element.38.mo_ref, bf16[512,1024]{1,0:T(8,128)(2,1)} %copy-done.14, f32[3,512,512]{2,1,0:T(8,128)} %get-tuple-element.41.refs_0_.f_ref, f32[512,512]{1,0:T(8,128)} %get-tuple-element.42.refs_1_.filt_ref, ...), custom_call_target="tpu_custom_call" | custom-call | flops 99999997952 | bytes 9437184 | tf_op jit(solution)/shard_map/backward/pallas_call | solution.py:236
  195.9 7.5 %all-to-all-done.2.refs_1_ = bf16[4,3,128,512]{3,2,1,0:T(8,128)(2,1)S(1)} async-done(((bf16[4,3,128,512]{3,2,1,0:T(8,128)(2,1)}), bf16[4,3,128,512]{3,2,1,0:T(8,128)(2,1)S(1)}, u32[]{:S(2)}, u32[]{:S(2)}) %all-to-all-start.2) | async-done | bytes 1572896 | tf_op jit(solution)/shard_map/all_to_all | solution.py:629
  203.5 3.6 %all-to-all-start.1 = ((bf16[4,3,128,512]{3,2,1,0:T(8,128)(2,1)}), bf16[4,3,128,512]{3,2,1,0:T(8,128)(2,1)S(1)}, u32[]{:S(2)}, u32[]{:S(2)}) async-start(bf16[4,3,128,512]{3,2,1,0:T(8,128)(2,1)} %get-tuple-element.48), calls=%async_computation.1 | async-start | bytes 3145728 | tf_op jit(solution)/shard_map/all_to_all | solution.py:629
  207.1 5.9 %collective-permute-done.9 = f32[32,1024]{1,0:T(8,128)S(1)} collective-permute-done((f32[32,1024]{1,0:T(8,128)S(1)}, f32[32,1024]{1,0:T(8,128)S(1)}, u32[]{:S(2)}, u32[]{:S(2)}) %collective-permute-start.9) | collective-permute-done | bytes 131104 | tf_op jit(solution)/shard_map/ppermute | solution.py:327
  213.0 8.7 %collective-permute-start.10 = (f32[32,1024]{1,0:T(8,128)S(1)}, f32[32,1024]{1,0:T(8,128)S(1)}, u32[]{:S(2)}, u32[]{:S(2)}) collective-permute-start(f32[32,1024]{1,0:T(8,128)S(1)} %fusion), channel_id=1, source_target_pairs={{0,8},{8,0},{16,24},{24,16},{1,9},{9,1},{17,25},{25,17},{2,10},{10... | collective-permute-start | bytes 393224 | tf_op jit(solution)/shard_map/ppermute | solution.py:327
  221.7 11.4 %collective-permute-done.10 = f32[32,1024]{1,0:T(8,128)S(1)} collective-permute-done((f32[32,1024]{1,0:T(8,128)S(1)}, f32[32,1024]{1,0:T(8,128)S(1)}, u32[]{:S(2)}, u32[]{:S(2)}) %collective-permute-start.10) | collective-permute-done | bytes 131104 | tf_op jit(solution)/shard_map/ppermute | solution.py:327
  233.1 3.7 %collective-permute-start.11 = (f32[32,1024]{1,0:T(8,128)S(1)}, f32[32,1024]{1,0:T(8,128)S(1)}, u32[]{:S(2)}, u32[]{:S(2)}) collective-permute-start(f32[32,1024]{1,0:T(8,128)S(1)} %add.20), channel_id=1, source_target_pairs={{0,16},{8,24},{16,0},{24,8},{1,17},{9,25},{17,1},{25,9},{2,18},{10... | collective-permute-start | bytes 393224 | tf_op jit(solution)/shard_map/ppermute | solution.py:327
  236.8 15.9 %collective-permute-done.11 = f32[32,1024]{1,0:T(8,128)S(1)} collective-permute-done((f32[32,1024]{1,0:T(8,128)S(1)}, f32[32,1024]{1,0:T(8,128)S(1)}, u32[]{:S(2)}, u32[]{:S(2)}) %collective-permute-start.11) | collective-permute-done | bytes 131104 | tf_op jit(solution)/shard_map/ppermute | solution.py:327
  255.2 4.2 %unpack.1 = (bf16[128,4096]{1,0:T(8,128)(2,1)}, bf16[128,4096]{1,0:T(8,128)(2,1)}, bf16[128,4096]{1,0:T(8,128)(2,1)}) custom-call(bf16[4,3,128,512]{3,2,1,0:T(8,128)(2,1)} %copy-done.3, bf16[4,3,128,512]{3,2,1,0:T(8,128)(2,1)} %copy-done.2), custom_call_target="tpu_custom_call" | custom-call | tf_op jit(solution)/shard_map/unpack/pallas_call | solution.py:305
  260.2 2.8 %convert_element_type.7 = f32[1024,512]{1,0:T(8,128)} convert(bf16[1024,512]{1,0:T(8,128)(2,1)} %reduce-scatter.2.cloned.1.call-done) | non-fusion elementwise | flops 524288 | bytes 3145728 | tf_op jit(solution)/shard_map/convert_element_type | solution.py:648
  (66 shorter events, 27.6 us)
Async XLA Ops:
  7.2 98.0 %all-gather.2.cloned.1.call-start = ((), (), s32[]{:S(2)}) async-start(), calls=%async_computation.4 | async-start | bytes 5242880 | tf_op jit(solution)/shard_map/all_gather | solution.py:584
  12.1 42.0 %all-to-all-start = ((bf16[4,3,128,1024]{3,2,1,0:T(8,128)(2,1)}), bf16[4,3,128,1024]{3,2,1,0:T(8,128)(2,1)S(1)}, u32[]{:S(2)}, u32[]{:S(2)}) async-start(bf16[4,3,128,1024]{3,2,1,0:T(8,128)(2,1)} %pack.1.refs_2_), calls=%async_computation | async-start | bytes 6291456 | tf_op jit(solution)/shard_map/all_to_all | solution.py:589
  16.3 243.9 %reduce-scatter.2.cloned.1.call-start = ((), (), s32[]{:S(2)}) async-start(), calls=%async_computation.5 | async-start | bytes 5242880 | tf_op jit(solution)/shard_map/reduce_scatter | solution.py:621
  16.3 24.6 %copy-start.10 = (f32[128,64]{0,1:T(8,128)S(1)}, f32[128,64]{0,1:T(8,128)}, u32[]{:S(2)}) copy-start(f32[128,64]{0,1:T(8,128)} %param.14) | copy-start | bytes 98308
  19.8 15.2 %collective-permute-start = (bf16[128,2048]{1,0:T(8,128)(2,1)}, bf16[128,2048]{1,0:T(8,128)(2,1)S(1)}, u32[]{:S(2)}, u32[]{:S(2)}) collective-permute-start(bf16[128,2048]{1,0:T(8,128)(2,1)} %get-tuple-element.33), channel_id=1, source_target_pairs={{0,4},{4,0},{1,5},{5,1},{2,6},{6,2},{3,7},{7,3},{8,12},{12,8},{9,1... | collective-permute-start | bytes 1572872 | tf_op jit(solution)/shard_map/ppermute | solution.py:323
  35.0 0.8 copy-start.7
  39.2 36.7 %collective-permute-start.1 = (bf16[2,1,128,2048]{3,2,1,0:T(8,128)(2,1)}, bf16[2,1,128,2048]{3,2,1,0:T(8,128)(2,1)}, u32[]{:S(2)}, u32[]{:S(2)}) collective-permute-start(bf16[2,1,128,2048]{3,2,1,0:T(8,128)(2,1)} %join.2.refs_1_.refs_0_), channel_id=1, source_target_pairs={{0,2},{1,3},{2,0},{3,1},{4,6},{5,7},{6,4},{7,5},{8,10},{9,11},{10,... | collective-permute-start | bytes 3145736 | tf_op jit(solution)/shard_map/ppermute | solution.py:327
  54.2 1.6 copy-start
  58.1 17.8 %collective-permute-start.2 = (bf16[176,1024]{1,0:T(8,128)(2,1)}, bf16[176,1024]{1,0:T(8,128)(2,1)S(1)}, u32[]{:S(2)}, u32[]{:S(2)}) collective-permute-start(bf16[176,1024]{1,0:T(8,128)(2,1)} %tail.1), channel_id=1, source_target_pairs={{0,4},{4,8},{8,12},{12,16},{16,20},{20,24},{24,28},{1,5},{5,9},{9,... | collective-permute-start | bytes 1081352 | tf_op jit(solution)/shard_map/ppermute | solution.py:318
  75.9 0.7 copy-start.4
  80.4 24.8 %collective-permute-start.3 = (bf16[2,2,128,2048]{3,2,1,0:T(8,128)(2,1)}, bf16[2,2,128,2048]{3,2,1,0:T(8,128)(2,1)S(1)}, u32[]{:S(2)}, u32[]{:S(2)}) collective-permute-start(bf16[2,2,128,2048]{3,2,1,0:T(8,128)(2,1)} %join.3._.a_ref), channel_id=1, source_target_pairs={{0,1},{1,0},{2,3},{3,2},{4,5},{5,4},{6,7},{7,6},{8,9},{9,8},{10,11... | collective-permute-start | bytes 6291464 | tf_op jit(solution)/shard_map/ppermute | solution.py:327
  88.3 16.8 %collective-permute-start.4 = (bf16[512,512]{1,0:T(8,128)(2,1)}, bf16[512,512]{1,0:T(8,128)(2,1)S(1)}, u32[]{:S(2)}, u32[]{:S(2)}) collective-permute-start(bf16[512,512]{1,0:T(8,128)(2,1)} %get-tuple-element.35._.refs_0_), channel_id=1, source_target_pairs={{0,4},{4,0},{1,5},{5,1},{2,6},{6,2},{3,7},{7,3},{8,12},{12,8},{9,1... | collective-permute-start | bytes 1572872 | tf_op jit(solution)/shard_map/ppermute | solution.py:323
  99.5 16.7 %collective-permute-start.5 = (bf16[512,512]{1,0:T(8,128)(2,1)}, bf16[512,512]{1,0:T(8,128)(2,1)S(1)}, u32[]{:S(2)}, u32[]{:S(2)}) collective-permute-start(bf16[512,512]{1,0:T(8,128)(2,1)} %get-tuple-element.36.refs_0_), channel_id=1, source_target_pairs={{0,4},{4,0},{1,5},{5,1},{2,6},{6,2},{3,7},{7,3},{8,12},{12,8},{9,1... | collective-permute-start | bytes 1572872 | tf_op jit(solution)/shard_map/ppermute | solution.py:323
  105.1 0.8 copy-start.5
  105.2 1.6 copy-start.1
  113.8 10.6 %collective-permute-start.6 = (bf16[144,1024]{1,0:T(8,128)(2,1)}, bf16[144,1024]{1,0:T(8,128)(2,1)S(1)}, u32[]{:S(2)}, u32[]{:S(2)}) collective-permute-start(bf16[144,1024]{1,0:T(8,128)(2,1)} %get-tuple-element.40), channel_id=1, source_target_pairs={{0,4},{4,0},{1,5},{5,1},{2,6},{6,2},{3,7},{7,3},{8,12},{12,8},{9,1... | collective-permute-start | bytes 884744 | tf_op jit(solution)/shard_map/ppermute | solution.py:323
  116.2 0.8 copy-start.6
  124.4 0.7 copy-start.9
  127.8 40.5 %collective-permute-start.7 = (bf16[512,1024]{1,0:T(8,128)(2,1)}, bf16[512,1024]{1,0:T(8,128)(2,1)S(1)}, u32[]{:S(2)}, u32[]{:S(2)}) collective-permute-start(bf16[512,1024]{1,0:T(8,128)(2,1)} %get-tuple-element.45), channel_id=1, source_target_pairs={{0,4},{4,0},{1,5},{5,1},{2,6},{6,2},{3,7},{7,3},{8,12},{12,8},{9,1... | collective-permute-start | bytes 3145736 | tf_op jit(solution)/shard_map/ppermute | solution.py:323
  129.6 31.9 %collective-permute-start.8 = (bf16[192,1024]{1,0:T(8,128)(2,1)}, bf16[192,1024]{1,0:T(8,128)(2,1)S(1)}, u32[]{:S(2)}, u32[]{:S(2)}) collective-permute-start(bf16[192,1024]{1,0:T(8,128)(2,1)} %get-tuple-element.46.refs_2_), channel_id=1, source_target_pairs={{4,0},{8,4},{12,8},{16,12},{20,16},{24,20},{28,24},{5,1},{9,5},{13... | collective-permute-start | bytes 1179656 | tf_op jit(solution)/shard_map/ppermute | solution.py:318
  161.4 0.8 copy-start.8
  168.3 1.0 copy-start.14
  179.8 23.6 %all-to-all-start.2 = ((bf16[4,3,128,512]{3,2,1,0:T(8,128)(2,1)}), bf16[4,3,128,512]{3,2,1,0:T(8,128)(2,1)S(1)}, u32[]{:S(2)}, u32[]{:S(2)}) async-start(bf16[4,3,128,512]{3,2,1,0:T(8,128)(2,1)} %get-tuple-element.49), calls=%async_computation.2 | async-start | bytes 3145728 | tf_op jit(solution)/shard_map/all_to_all | solution.py:629
  183.4 10.9 %copy-start.13 = (f32[32,128]{1,0:T(8,128)S(1)}, f32[32,128]{1,0:T(8,128)}, u32[]{:S(2)}) copy-start(f32[32,128]{1,0:T(8,128)} %get-tuple-element.56) | copy-start | bytes 49156
  183.4 11.7 %copy-start.12 = (f32[3,8,512]{2,1,0:T(8,128)S(1)}, f32[3,8,512]{2,1,0:T(8,128)}, u32[]{:S(2)}) copy-start(f32[3,8,512]{2,1,0:T(8,128)} %get-tuple-element.54) | copy-start | bytes 147460
  203.5 50.6 %copy-start.2 = (bf16[4,3,128,512]{3,2,1,0:T(8,128)(2,1)}, bf16[4,3,128,512]{3,2,1,0:T(8,128)(2,1)S(1)}, u32[]{:S(2)}) copy-start(bf16[4,3,128,512]{3,2,1,0:T(8,128)(2,1)S(1)} %all-to-all-done.2.refs_1_) | copy-start | bytes 4718596
  203.5 50.6 %all-to-all-start.1 = ((bf16[4,3,128,512]{3,2,1,0:T(8,128)(2,1)}), bf16[4,3,128,512]{3,2,1,0:T(8,128)(2,1)S(1)}, u32[]{:S(2)}, u32[]{:S(2)}) async-start(bf16[4,3,128,512]{3,2,1,0:T(8,128)(2,1)} %get-tuple-element.48), calls=%async_computation.1 | async-start | bytes 3145728 | tf_op jit(solution)/shard_map/all_to_all | solution.py:629
  207.0 5.9 %collective-permute-start.9 = (f32[32,1024]{1,0:T(8,128)S(1)}, f32[32,1024]{1,0:T(8,128)S(1)}, u32[]{:S(2)}, u32[]{:S(2)}) collective-permute-start(f32[32,1024]{1,0:T(8,128)S(1)} %pad_maximum_fusion), channel_id=1, source_target_pairs={{0,4},{4,0},{1,5},{5,1},{2,6},{6,2},{3,7},{7,3},{8,12},{12,8},{9,1... | collective-permute-start | bytes 393224 | tf_op jit(solution)/shard_map/ppermute | solution.py:327
  213.0 20.1 %collective-permute-start.10 = (f32[32,1024]{1,0:T(8,128)S(1)}, f32[32,1024]{1,0:T(8,128)S(1)}, u32[]{:S(2)}, u32[]{:S(2)}) collective-permute-start(f32[32,1024]{1,0:T(8,128)S(1)} %fusion), channel_id=1, source_target_pairs={{0,8},{8,0},{16,24},{24,16},{1,9},{9,1},{17,25},{25,17},{2,10},{10... | collective-permute-start | bytes 393224 | tf_op jit(solution)/shard_map/ppermute | solution.py:327
  233.1 19.6 %collective-permute-start.11 = (f32[32,1024]{1,0:T(8,128)S(1)}, f32[32,1024]{1,0:T(8,128)S(1)}, u32[]{:S(2)}, u32[]{:S(2)}) collective-permute-start(f32[32,1024]{1,0:T(8,128)S(1)} %add.20), channel_id=1, source_target_pairs={{0,16},{8,24},{16,0},{24,8},{1,17},{9,25},{17,1},{25,9},{2,18},{10... | collective-permute-start | bytes 393224 | tf_op jit(solution)/shard_map/ppermute | solution.py:327
  253.4 9.6 %copy-start.11 = (f32[3,8,1024]{2,1,0:T(8,128)}, f32[3,8,1024]{2,1,0:T(8,128)S(1)}, u32[]{:S(2)}) copy-start(f32[3,8,1024]{2,1,0:T(8,128)S(1)} %slice_bitcast_fusion) | copy-start | bytes 294916
  254.1 1.1 copy-start.3
Sparse Core Ops, SparseCore 0:
  9.6 83.4 all-gather.1
  168.4 91.7 reduce-scatter.1

commit v3 on v2

--- a/solution.py
+++ b/solution.py
@@ -525,7 +525,7 @@
 
 
 def head_kernel(chunks, mo_ref, mr_ref, *refs):
-    out_ref = refs[-2]
+    out_ref = refs[-1]
     edge = LTAPS + PAD
     part = out_ref.shape[1] // chunks
     for h in range(chunks):
@@ -538,7 +538,7 @@
         out_ref[edge + 2 * PAD :, own] = (mixed[0:PAD] * filt_ref[0:PAD]).astype(BF16)
 
 
-def head_of(mixed_own, mixed_rest, mixers, passed):
+def head_of(mixed_own, mixed_rest, mixers):
     edge, cols = LTAPS + PAD, mixed_own.shape[1]
     part = cols // len(mixers)
     whole = pl.BlockSpec((edge, cols), lambda i: (0, 0))
@@ -549,16 +549,27 @@
     return pl.pallas_call(
         functools.partial(head_kernel, len(mixers)),
         grid=(1,),
-        in_specs=[whole, whole] + feat_specs * len(mixers) + [pl.BlockSpec(memory_space=pl.ANY)],
-        out_specs=[pl.BlockSpec((edge + 3 * PAD, cols), lambda i: (0, 0)), pl.BlockSpec(memory_space=pl.ANY)],
-        out_shape=[
-            jax.ShapeDtypeStruct((edge + 3 * PAD, cols), BF16),
-            jax.ShapeDtypeStruct(passed.shape, passed.dtype),
-        ],
-        input_output_aliases={2 + 2 * len(mixers): 1},
+        in_specs=[whole, whole] + feat_specs * len(mixers),
+        out_specs=pl.BlockSpec((edge + 3 * PAD, cols), lambda i: (0, 0)),
+        out_shape=jax.ShapeDtypeStruct((edge + 3 * PAD, cols), BF16),
         compiler_params=params(),
         name="head",
-    )(mixed_own, mixed_rest, *[array for mixer in mixers for array in mixer[1:]], passed)
+    )(mixed_own, mixed_rest, *[array for mixer in mixers for array in mixer[1:]])
+
+
+def pass_kernel(*_):
+    pass
+
+
+def pass_after(value, after):
+    return pl.pallas_call(
+        pass_kernel,
+        in_specs=[pl.BlockSpec(memory_space=pl.ANY)] * 2,
+        out_specs=pl.BlockSpec(memory_space=pl.ANY),
+        out_shape=jax.ShapeDtypeStruct(value.shape, value.dtype),
+        input_output_aliases={0: 0},
+        name="pass_after",
+    )(value, after)
 
 
 def contract(a, b, dim):
@@ -609,10 +620,11 @@
         heads.append(around(head, "y", -step))
     mixed_own, own_head = mixed_grad(cots, weights, place, 0, F32, [parts[-1], *mixed_all[-1][1:]])
     head_rest = heads[0] if len(heads) == 1 else sum(piece.astype(F32) for piece in heads)
-    head, parts[-1] = head_of(own_head, head_rest, mixers, parts[-1])
+    head = head_of(own_head, head_rest, mixers)
+    later = along(head, fsdp, -1)
+    parts[-1] = pass_after(parts[-1], later)
     rest = [around(parts[step - 1], "y", -step) for step in range(1, ys)]
     mixed_rest = rest[0] if len(rest) == 1 else sum(piece.astype(F32) for piece in rest)
-    later = along(head, fsdp, -1)
 
     weight_sum = None
     for h in range(chunks):

time: 272 us -> 265 us (0.974)
  waiting for transfers between devices: 105 us -> 96.5 us
    ppermute x2, waiting for transfers between devices: 24.6 us -> 11.8 us  [along(): lax.ppermute(block, axis, [(i, i + distance) for i in range(size) if 0 <=...]
    ppermute x5, waiting for transfers between devices: 18.8 us -> 29.6 us  [around(): lax.ppermute(block, axis, [(i, (i + distance) % size) for i in range(size)])]
    ppermute x5, starting transfers between devices: 10.1 us -> 16.7 us  [around(): lax.ppermute(block, axis, [(i, (i + distance) % size) for i in range(size)])]
    ppermute x5, waiting for transfers between devices: 47.1 us -> 41.3 us  [across(): lax.ppermute(block, axis, [(i, i ^ bit) for i in range(lax.axis_size(axis...]
    ppermute x5, starting transfers between devices: 14.1 us -> 9.19 us  [across(): lax.ppermute(block, axis, [(i, i ^ bit) for i in range(lax.axis_size(axis...]
where the time goes in v3:
time: 265 us; the launch traced here: 263 us
  waiting for transfers between devices  96.5 us (36%)
  Pallas kernels  93 us (35%)
  starting transfers between devices  42.5 us (16%)
  between operations  14.2 us (5%)
  local copies, waits for them, and re-layouts  11.8 us (4%)
  other arithmetic  4.95 us (2%)
    ppermute x5, waiting for transfers between devices, across(): lax.ppermute(block, axis, [(i, i ^ bit) for i in range(lax.axis_size(axis...  41.3 us
    ppermute x5, waiting for transfers between devices, around(): lax.ppermute(block, axis, [(i, (i + distance) % size) for i in range(size)])  29.6 us
    pallas_call x2, Pallas kernels, backward(): pl.pallas_call(backward_kernel, grid=(tiles,), in_specs=[tok, tok, pl.Blo...  21.1 us
    ppermute x5, starting transfers between devices, around(): lax.ppermute(block, axis, [(i, (i + distance) % size) for i in range(size)])  16.7 us
    pallas_call x2, Pallas kernels, forward(): pl.pallas_call(forward_kernel, grid_spec=pltpu.PrefetchScalarGridSpec(num...  14.8 us
    pallas_call x2, Pallas kernels, mixed_grad(): pl.pallas_call(functools.partial(mixed_grad_kernel, len(after)), grid_spe...  14.4 us
    pallas_call x2, Pallas kernels, weight_grad(): pl.pallas_call(functools.partial(weight_grad_kernel, scale), grid=(Z,), i...  12 us
    ppermute x2, waiting for transfers between devices, along(): lax.ppermute(block, axis, [(i, i + distance) for i in range(size) if 0 <=...  11.8 us
  transfers between devices with their start and end apart: 17, of which 11 were waited for; matrix products, arithmetic and copies ran while one was open for 2% of the time, Pallas kernels for 34%

profile of v3, /device:TPU:0, one launch (start us, length us, event | category | flops | bytes accessed | tf_op | source)
XLA Modules:
  0.0 262.8 jit_solution(8583043884764671280)
XLA Ops:
  7.9 4.2 %pack.1.refs_2_ = bf16[4,3,128,1024]{3,2,1,0:T(8,128)(2,1)} custom-call(bf16[128,4096]{1,0:T(8,128)(2,1)} %refs_0_.2, bf16[128,4096]{1,0:T(8,128)(2,1)} %refs_1_.2, bf16[128,4096]{1,0:T(8,128)(2,1)} %refs_2_.1), custom_call_target="tpu_custom_call" | custom-call | tf_op jit(solution)/shard_map/pack/pallas_call | solution.py:282
  12.1 4.2 %all-to-all-start = ((bf16[4,3,128,1024]{3,2,1,0:T(8,128)(2,1)}), bf16[4,3,128,1024]{3,2,1,0:T(8,128)(2,1)S(1)}, u32[]{:S(2)}, u32[]{:S(2)}) async-start(bf16[4,3,128,1024]{3,2,1,0:T(8,128)(2,1)} %pack.1.refs_2_), calls=%async_computation | async-start | bytes 6291456 | tf_op jit(solution)/shard_map/all_to_all | solution.py:600
  16.3 3.5 %split.1 = (bf16[128,2048]{1,0:T(8,128)(2,1)}, bf16[128,2048]{1,0:T(8,128)(2,1)}) custom-call(s32[1]{0:T(128)} %bitcast.y_ref, bf16[128,4096]{1,0:T(8,128)(2,1)} %refs_1_.3, bf16[128,4096]{1,0:T(8,128)(2,1)} %refs_1_.3, bf16[4,3,128,1024]{3,2,1,0:T(8,128)(2,1)} %pack.1.refs_2_), custom_call_target="tpu_custom_call" | custom-call | tf_op jit(solution)/shard_map/split/pallas_call | solution.py:354
  22.3 12.7 %collective-permute-done = bf16[128,2048]{1,0:T(8,128)(2,1)S(1)} collective-permute-done((bf16[128,2048]{1,0:T(8,128)(2,1)}, bf16[128,2048]{1,0:T(8,128)(2,1)S(1)}, u32[]{:S(2)}, u32[]{:S(2)}) %collective-permute-start) | collective-permute-done | bytes 524320 | tf_op jit(solution)/shard_map/ppermute | solution.py:323
  35.8 3.4 %join.2.refs_1_.refs_0_ = bf16[2,1,128,2048]{3,2,1,0:T(8,128)(2,1)} custom-call(bf16[1,1,128,2048]{3,2,1,0:T(8,128)(2,1)} %bitcast.12, bf16[1,1,128,2048]{3,2,1,0:T(8,128)(2,1)} %bitcast.13), custom_call_target="tpu_custom_call" | custom-call | tf_op jit(solution)/shard_map/join/pallas_call | solution.py:384
  42.3 6.7 %tables.1 = (bf16[8192,256]{1,0:T(8,128)(2,1)}, bf16[8192,256]{1,0:T(8,128)(2,1)}) custom-call(f32[64,256]{1,0:T(8,128)} %pad.8.fwd_ref, f32[64,256]{1,0:T(8,128)} %pad.9.bwd_ref), custom_call_target="tpu_custom_call" | custom-call | tf_op jit(solution)/shard_map/tables/pallas_call | solution.py:41
  49.0 5.2 %all-to-all-done.x_ref.before_ref = bf16[4,3,128,1024]{3,2,1,0:T(8,128)(2,1)S(1)} async-done(((bf16[4,3,128,1024]{3,2,1,0:T(8,128)(2,1)}), bf16[4,3,128,1024]{3,2,1,0:T(8,128)(2,1)S(1)}, u32[]{:S(2)}, u32[]{:S(2)}) %all-to-all-start) | async-done | bytes 3145760 | tf_op jit(solution)/shard_map/all_to_all | solution.py:600
  58.1 3.9 %collective-permute-start.2 = (bf16[176,1024]{1,0:T(8,128)(2,1)}, bf16[176,1024]{1,0:T(8,128)(2,1)S(1)}, u32[]{:S(2)}, u32[]{:S(2)}) collective-permute-start(bf16[176,1024]{1,0:T(8,128)(2,1)} %tail.1), channel_id=1, source_target_pairs={{0,4},{4,8},{8,12},{12,16},{16,20},{20,24},{24,28},{1,5},{5,9},{9,... | collective-permute-start | bytes 1081352 | tf_op jit(solution)/shard_map/ppermute | solution.py:318
  62.0 13.9 %collective-permute-done.1.refs_1_ = bf16[2,1,128,2048]{3,2,1,0:T(8,128)(2,1)} collective-permute-done((bf16[2,1,128,2048]{3,2,1,0:T(8,128)(2,1)}, bf16[2,1,128,2048]{3,2,1,0:T(8,128)(2,1)}, u32[]{:S(2)}, u32[]{:S(2)}) %collective-permute-start.1) | collective-permute-done | bytes 1048608 | tf_op jit(solution)/shard_map/ppermute | solution.py:327
  76.6 3.8 %join.3._.a_ref = bf16[2,2,128,2048]{3,2,1,0:T(8,128)(2,1)} custom-call(bf16[2,1,128,2048]{3,2,1,0:T(8,128)(2,1)} %join.2.refs_1_.refs_0_, bf16[2,1,128,2048]{3,2,1,0:T(8,128)(2,1)} %collective-permute-done.1.refs_1_, bf16[176,1024]{1,0:T(8,128)(2,1)} %copy-done.4), custom_call_target="tpu_custom_call" | custom-call | tf_op jit(solution)/shard_map/join/pallas_call | solution.py:384
  80.9 7.4 %forward.2 = (bf16[512,512]{1,0:T(8,128)(2,1)}, f32[3,512,512]{2,1,0:T(8,128)}, f32[512,512]{1,0:T(8,128)}) custom-call(s32[4]{0:T(128)} %shift-left_add_fusion.place_ref, bf16[4,3,128,1024]{3,2,1,0:T(8,128)(2,1)} %copy-done, bf16[176,1024]{1,0:T(8,128)(2,1)} %copy-done.4, f32[3,7,1024]{2,1,0:T(8,128)} %taps_ref.9, f32[1,1024]{1,0:T(1,128)} %bitcast.18, ...), custom_call_target="tpu_custom_call" | custom-call | tf_op jit(solution)/shard_map/forward/pallas_call | solution.py:111
  88.3 3.8 %collective-permute-start.4 = (bf16[512,512]{1,0:T(8,128)(2,1)}, bf16[512,512]{1,0:T(8,128)(2,1)S(1)}, u32[]{:S(2)}, u32[]{:S(2)}) collective-permute-start(bf16[512,512]{1,0:T(8,128)(2,1)} %get-tuple-element.33._.refs_0_), channel_id=1, source_target_pairs={{0,4},{4,0},{1,5},{5,1},{2,6},{6,2},{3,7},{7,3},{8,12},{12,8},{9,1... | collective-permute-start | bytes 1572872 | tf_op jit(solution)/shard_map/ppermute | solution.py:323
  92.1 7.4 %forward.3 = (bf16[512,512]{1,0:T(8,128)(2,1)}, f32[3,512,512]{2,1,0:T(8,128)}, f32[512,512]{1,0:T(8,128)}) custom-call(s32[4]{0:T(128)} %shift-left_add_fusion.place_ref, bf16[4,3,128,1024]{3,2,1,0:T(8,128)(2,1)} %copy-done, bf16[176,1024]{1,0:T(8,128)(2,1)} %copy-done.4, f32[3,7,1024]{2,1,0:T(8,128)} %taps_ref.9, f32[1,1024]{1,0:T(1,128)} %bitcast.19, ...), custom_call_target="tpu_custom_call" | custom-call | tf_op jit(solution)/shard_map/forward/pallas_call | solution.py:111
  99.5 5.6 %collective-permute-done.4.refs_1_ = bf16[512,512]{1,0:T(8,128)(2,1)S(1)} collective-permute-done((bf16[512,512]{1,0:T(8,128)(2,1)}, bf16[512,512]{1,0:T(8,128)(2,1)S(1)}, u32[]{:S(2)}, u32[]{:S(2)}) %collective-permute-start.4) | collective-permute-done | bytes 524320 | tf_op jit(solution)/shard_map/ppermute | solution.py:323
  106.7 7.1 %mixed_grad.2 = (bf16[512,1024]{1,0:T(8,128)(2,1)}, bf16[144,1024]{1,0:T(8,128)(2,1)}) custom-call(s32[4]{0:T(128)} %shift-left_add_fusion.place_ref, bf16[2,2,128,2048]{3,2,1,0:T(8,128)(2,1)} %join.3._.a_ref, bf16[2,2,128,2048]{3,2,1,0:T(8,128)(2,1)} %copy-done.1, bf16[1024,2048]{1,0:T(8,128)(2,1)} %all-gather.2.cloned.1.call-done.w_ref, ...), custom_call_target="tpu_custom_call" | custom-call | tf_op jit(solution)/shard_map/mixed_grad/pallas_call | solution.py:428
  117.0 7.4 %mixed_grad.3 = (f32[512,1024]{1,0:T(8,128)}, f32[144,1024]{1,0:T(8,128)}) custom-call(s32[4]{0:T(128)} %shift-left_add_fusion.place_ref, bf16[2,2,128,2048]{3,2,1,0:T(8,128)(2,1)} %join.3._.a_ref, bf16[2,2,128,2048]{3,2,1,0:T(8,128)(2,1)} %copy-done.1, bf16[1024,2048]{1,0:T(8,128)(2,1)} %all-gather.2.cloned.1.call-done.w_ref, ...), custom_call_target="tpu_custom_call" | custom-call | tf_op jit(solution)/shard_map/mixed_grad/pallas_call | solution.py:428
  129.1 11.8 %collective-permute-done.7.__1_.n_ref.refs_2_ = bf16[192,1024]{1,0:T(8,128)(2,1)S(1)} collective-permute-done((bf16[192,1024]{1,0:T(8,128)(2,1)}, bf16[192,1024]{1,0:T(8,128)(2,1)S(1)}, u32[]{:S(2)}, u32[]{:S(2)}) %collective-permute-start.7) | collective-permute-done | bytes 393248 | tf_op jit(solution)/shard_map/ppermute | solution.py:318
  141.6 8.3 %collective-permute-start.8 = (bf16[512,1024]{1,0:T(8,128)(2,1)}, bf16[512,1024]{1,0:T(8,128)(2,1)S(1)}, u32[]{:S(2)}, u32[]{:S(2)}) collective-permute-start(bf16[512,1024]{1,0:T(8,128)(2,1)} %pass_after.1), channel_id=1, source_target_pairs={{0,4},{4,0},{1,5},{5,1},{2,6},{6,2},{3,7},{7,3},{8,12},{12,8},{9,1... | collective-permute-start | bytes 3145736 | tf_op jit(solution)/shard_map/ppermute | solution.py:323
  149.9 6.0 %weight_grad.2.refs_3_ = bf16[1024,2048]{1,0:T(8,128)(2,1)} custom-call(bf16[2,2,128,2048]{3,2,1,0:T(8,128)(2,1)} %join.3._.a_ref, bf16[2,2,128,2048]{3,2,1,0:T(8,128)(2,1)} %copy-done.1, bf16[512,512]{1,0:T(8,128)(2,1)} %get-tuple-element.33._.refs_0_, bf16[512,512]{1,0:T(8,128)(2,1)} %copy-done.5, bf16[192,1024]{1,0:T(8,128)(2,1)} %head.1.refs_2_), custom_call_target="tpu_custom_call" | custom-call | tf_op jit(solution)/shard_map/weight_grad/pallas_call | solution.py:473
  155.9 6.0 %weight_grad.3 = bf16[1024,2048]{1,0:T(8,128)(2,1)} custom-call(bf16[2,2,128,2048]{3,2,1,0:T(8,128)(2,1)} %join.3._.a_ref, bf16[2,2,128,2048]{3,2,1,0:T(8,128)(2,1)} %copy-done.1, bf16[512,512]{1,0:T(8,128)(2,1)} %get-tuple-element.34.refs_0_, bf16[512,512]{1,0:T(8,128)(2,1)} %copy-done.6, ...), custom_call_target="tpu_custom_call", output_to_operand_aliasing={{}: (5, {})} | custom-call | tf_op jit(solution)/shard_map/weight_grad/pallas_call | solution.py:473
  162.0 10.9 %collective-permute-done.8.mr_ref = bf16[512,1024]{1,0:T(8,128)(2,1)S(1)} collective-permute-done((bf16[512,1024]{1,0:T(8,128)(2,1)}, bf16[512,1024]{1,0:T(8,128)(2,1)S(1)}, u32[]{:S(2)}, u32[]{:S(2)}) %collective-permute-start.8) | collective-permute-done | bytes 1048608 | tf_op jit(solution)/shard_map/ppermute | solution.py:323
  173.8 10.6 %backward.3 = (bf16[4,3,128,512]{3,2,1,0:T(8,128)(2,1)}, f32[3,8,512]{2,1,0:T(8,128)}, f32[32,128]{1,0:T(8,128)}) custom-call(f32[512,1024]{1,0:T(8,128)} %get-tuple-element.36.mo_ref, bf16[512,1024]{1,0:T(8,128)(2,1)} %copy-done.14, f32[3,512,512]{2,1,0:T(8,128)} %get-tuple-element.41.refs_2_.f_ref, f32[512,512]{1,0:T(8,128)} %get-tuple-element.42.refs_3_.filt_ref, ...), custom_call_target="tpu_custom_call" | custom-call | flops 99999997952 | bytes 9437184 | tf_op jit(solution)/shard_map/backward/pallas_call | solution.py:236
  184.4 3.6 %all-to-all-start.2 = ((bf16[4,3,128,512]{3,2,1,0:T(8,128)(2,1)}), bf16[4,3,128,512]{3,2,1,0:T(8,128)(2,1)S(1)}, u32[]{:S(2)}, u32[]{:S(2)}) async-start(bf16[4,3,128,512]{3,2,1,0:T(8,128)(2,1)} %get-tuple-element.45), calls=%async_computation.2 | async-start | bytes 3145728 | tf_op jit(solution)/shard_map/all_to_all | solution.py:641
  188.0 10.5 %backward.2 = (bf16[4,3,128,512]{3,2,1,0:T(8,128)(2,1)}, f32[3,8,512]{2,1,0:T(8,128)}, f32[32,128]{1,0:T(8,128)}) custom-call(f32[512,1024]{1,0:T(8,128)} %get-tuple-element.36.mo_ref, bf16[512,1024]{1,0:T(8,128)(2,1)} %copy-done.14, f32[3,512,512]{2,1,0:T(8,128)} %get-tuple-element.39.refs_0_.f_ref, f32[512,512]{1,0:T(8,128)} %get-tuple-element.40.refs_1_.filt_ref, ...), custom_call_target="tpu_custom_call" | custom-call | flops 99999997952 | bytes 9437184 | tf_op jit(solution)/shard_map/backward/pallas_call | solution.py:236
  200.1 8.0 %all-to-all-done.2.refs_1_ = bf16[4,3,128,512]{3,2,1,0:T(8,128)(2,1)S(1)} async-done(((bf16[4,3,128,512]{3,2,1,0:T(8,128)(2,1)}), bf16[4,3,128,512]{3,2,1,0:T(8,128)(2,1)S(1)}, u32[]{:S(2)}, u32[]{:S(2)}) %all-to-all-start.2) | async-done | bytes 1572896 | tf_op jit(solution)/shard_map/all_to_all | solution.py:641
  208.0 3.6 %all-to-all-start.1 = ((bf16[4,3,128,512]{3,2,1,0:T(8,128)(2,1)}), bf16[4,3,128,512]{3,2,1,0:T(8,128)(2,1)S(1)}, u32[]{:S(2)}, u32[]{:S(2)}) async-start(bf16[4,3,128,512]{3,2,1,0:T(8,128)(2,1)} %get-tuple-element.44), calls=%async_computation.1 | async-start | bytes 3145728 | tf_op jit(solution)/shard_map/all_to_all | solution.py:641
  213.4 4.1 %collective-permute-done.9 = f32[32,1024]{1,0:T(8,128)S(1)} collective-permute-done((f32[32,1024]{1,0:T(8,128)S(1)}, f32[32,1024]{1,0:T(8,128)S(1)}, u32[]{:S(2)}, u32[]{:S(2)}) %collective-permute-start.9) | collective-permute-done | bytes 131104 | tf_op jit(solution)/shard_map/ppermute | solution.py:327
  217.6 3.1 %collective-permute-start.10 = (f32[32,1024]{1,0:T(8,128)S(1)}, f32[32,1024]{1,0:T(8,128)S(1)}, u32[]{:S(2)}, u32[]{:S(2)}) collective-permute-start(f32[32,1024]{1,0:T(8,128)S(1)} %fusion), channel_id=1, source_target_pairs={{0,8},{8,0},{16,24},{24,16},{1,9},{9,1},{17,25},{25,17},{2,10},{10... | collective-permute-start | bytes 393224 | tf_op jit(solution)/shard_map/ppermute | solution.py:327
  220.7 10.6 %collective-permute-done.10 = f32[32,1024]{1,0:T(8,128)S(1)} collective-permute-done((f32[32,1024]{1,0:T(8,128)S(1)}, f32[32,1024]{1,0:T(8,128)S(1)}, u32[]{:S(2)}, u32[]{:S(2)}) %collective-permute-start.10) | collective-permute-done | bytes 131104 | tf_op jit(solution)/shard_map/ppermute | solution.py:327
  233.9 12.7 %collective-permute-done.11 = f32[32,1024]{1,0:T(8,128)S(1)} collective-permute-done((f32[32,1024]{1,0:T(8,128)S(1)}, f32[32,1024]{1,0:T(8,128)S(1)}, u32[]{:S(2)}, u32[]{:S(2)}) %collective-permute-start.11) | collective-permute-done | bytes 131104 | tf_op jit(solution)/shard_map/ppermute | solution.py:327
  249.0 4.2 %unpack.1 = (bf16[128,4096]{1,0:T(8,128)(2,1)}, bf16[128,4096]{1,0:T(8,128)(2,1)}, bf16[128,4096]{1,0:T(8,128)(2,1)}) custom-call(bf16[4,3,128,512]{3,2,1,0:T(8,128)(2,1)} %copy-done.3, bf16[4,3,128,512]{3,2,1,0:T(8,128)(2,1)} %copy-done.2), custom_call_target="tpu_custom_call" | custom-call | tf_op jit(solution)/shard_map/unpack/pallas_call | solution.py:305
  253.1 2.8 %convert_element_type.7 = f32[1024,512]{1,0:T(8,128)} convert(bf16[1024,512]{1,0:T(8,128)(2,1)} %reduce-scatter.2.cloned.1.call-done) | non-fusion elementwise | flops 524288 | bytes 3145728 | tf_op jit(solution)/shard_map/convert_element_type | solution.py:660
  (67 shorter events, 32.0 us)
Async XLA Ops:
  7.2 98.0 %all-gather.2.cloned.1.call-start = ((), (), s32[]{:S(2)}) async-start(), calls=%async_computation.4 | async-start | bytes 5242880 | tf_op jit(solution)/shard_map/all_gather | solution.py:595
  12.1 42.0 %all-to-all-start = ((bf16[4,3,128,1024]{3,2,1,0:T(8,128)(2,1)}), bf16[4,3,128,1024]{3,2,1,0:T(8,128)(2,1)S(1)}, u32[]{:S(2)}, u32[]{:S(2)}) async-start(bf16[4,3,128,1024]{3,2,1,0:T(8,128)(2,1)} %pack.1.refs_2_), calls=%async_computation | async-start | bytes 6291456 | tf_op jit(solution)/shard_map/all_to_all | solution.py:600
  16.3 236.8 %reduce-scatter.2.cloned.1.call-start = ((), (), s32[]{:S(2)}) async-start(), calls=%async_computation.5 | async-start | bytes 5242880 | tf_op jit(solution)/shard_map/reduce_scatter | solution.py:633
  16.3 24.6 %copy-start.10 = (f32[128,64]{0,1:T(8,128)S(1)}, f32[128,64]{0,1:T(8,128)}, u32[]{:S(2)}) copy-start(f32[128,64]{0,1:T(8,128)} %param.14) | copy-start | bytes 98308
  19.8 15.2 %collective-permute-start = (bf16[128,2048]{1,0:T(8,128)(2,1)}, bf16[128,2048]{1,0:T(8,128)(2,1)S(1)}, u32[]{:S(2)}, u32[]{:S(2)}) collective-permute-start(bf16[128,2048]{1,0:T(8,128)(2,1)} %get-tuple-element.31), channel_id=1, source_target_pairs={{0,4},{4,0},{1,5},{5,1},{2,6},{6,2},{3,7},{7,3},{8,12},{12,8},{9,1... | collective-permute-start | bytes 1572872 | tf_op jit(solution)/shard_map/ppermute | solution.py:323
  35.0 0.8 copy-start.8
  39.2 36.7 %collective-permute-start.1 = (bf16[2,1,128,2048]{3,2,1,0:T(8,128)(2,1)}, bf16[2,1,128,2048]{3,2,1,0:T(8,128)(2,1)}, u32[]{:S(2)}, u32[]{:S(2)}) collective-permute-start(bf16[2,1,128,2048]{3,2,1,0:T(8,128)(2,1)} %join.2.refs_1_.refs_0_), channel_id=1, source_target_pairs={{0,2},{1,3},{2,0},{3,1},{4,6},{5,7},{6,4},{7,5},{8,10},{9,11},{10,... | collective-permute-start | bytes 3145736 | tf_op jit(solution)/shard_map/ppermute | solution.py:327
  54.2 1.6 copy-start
  58.1 17.8 %collective-permute-start.2 = (bf16[176,1024]{1,0:T(8,128)(2,1)}, bf16[176,1024]{1,0:T(8,128)(2,1)S(1)}, u32[]{:S(2)}, u32[]{:S(2)}) collective-permute-start(bf16[176,1024]{1,0:T(8,128)(2,1)} %tail.1), channel_id=1, source_target_pairs={{0,4},{4,8},{8,12},{12,16},{16,20},{20,24},{24,28},{1,5},{5,9},{9,... | collective-permute-start | bytes 1081352 | tf_op jit(solution)/shard_map/ppermute | solution.py:318
  75.9 0.7 copy-start.4
  80.4 24.7 %collective-permute-start.3 = (bf16[2,2,128,2048]{3,2,1,0:T(8,128)(2,1)}, bf16[2,2,128,2048]{3,2,1,0:T(8,128)(2,1)S(1)}, u32[]{:S(2)}, u32[]{:S(2)}) collective-permute-start(bf16[2,2,128,2048]{3,2,1,0:T(8,128)(2,1)} %join.3._.a_ref), channel_id=1, source_target_pairs={{0,1},{1,0},{2,3},{3,2},{4,5},{5,4},{6,7},{7,6},{8,9},{9,8},{10,11... | collective-permute-start | bytes 6291464 | tf_op jit(solution)/shard_map/ppermute | solution.py:327
  88.3 16.8 %collective-permute-start.4 = (bf16[512,512]{1,0:T(8,128)(2,1)}, bf16[512,512]{1,0:T(8,128)(2,1)S(1)}, u32[]{:S(2)}, u32[]{:S(2)}) collective-permute-start(bf16[512,512]{1,0:T(8,128)(2,1)} %get-tuple-element.33._.refs_0_), channel_id=1, source_target_pairs={{0,4},{4,0},{1,5},{5,1},{2,6},{6,2},{3,7},{7,3},{8,12},{12,8},{9,1... | collective-permute-start | bytes 1572872 | tf_op jit(solution)/shard_map/ppermute | solution.py:323
  99.5 16.6 %collective-permute-start.5 = (bf16[512,512]{1,0:T(8,128)(2,1)}, bf16[512,512]{1,0:T(8,128)(2,1)S(1)}, u32[]{:S(2)}, u32[]{:S(2)}) collective-permute-start(bf16[512,512]{1,0:T(8,128)(2,1)} %get-tuple-element.34.refs_0_), channel_id=1, source_target_pairs={{0,4},{4,0},{1,5},{5,1},{2,6},{6,2},{3,7},{7,3},{8,12},{12,8},{9,1... | collective-permute-start | bytes 1572872 | tf_op jit(solution)/shard_map/ppermute | solution.py:323
  105.1 0.8 copy-start.5
  105.1 1.5 copy-start.1
  113.7 10.6 %collective-permute-start.6 = (bf16[144,1024]{1,0:T(8,128)(2,1)}, bf16[144,1024]{1,0:T(8,128)(2,1)S(1)}, u32[]{:S(2)}, u32[]{:S(2)}) collective-permute-start(bf16[144,1024]{1,0:T(8,128)(2,1)} %get-tuple-element.38), channel_id=1, source_target_pairs={{0,4},{4,0},{1,5},{5,1},{2,6},{6,2},{3,7},{7,3},{8,12},{12,8},{9,1... | collective-permute-start | bytes 884744 | tf_op jit(solution)/shard_map/ppermute | solution.py:323
  116.2 0.8 copy-start.6
  124.3 0.7 copy-start.9
  127.8 13.0 %collective-permute-start.7 = (bf16[192,1024]{1,0:T(8,128)(2,1)}, bf16[192,1024]{1,0:T(8,128)(2,1)S(1)}, u32[]{:S(2)}, u32[]{:S(2)}) collective-permute-start(bf16[192,1024]{1,0:T(8,128)(2,1)} %head.1.refs_2_), channel_id=1, source_target_pairs={{4,0},{8,4},{12,8},{16,12},{20,16},{24,20},{28,24},{5,1},{9,5},{13... | collective-permute-start | bytes 1179656 | tf_op jit(solution)/shard_map/ppermute | solution.py:318
  140.8 0.8 copy-start.7
  141.6 31.3 %collective-permute-start.8 = (bf16[512,1024]{1,0:T(8,128)(2,1)}, bf16[512,1024]{1,0:T(8,128)(2,1)S(1)}, u32[]{:S(2)}, u32[]{:S(2)}) collective-permute-start(bf16[512,1024]{1,0:T(8,128)(2,1)} %pass_after.1), channel_id=1, source_target_pairs={{0,4},{4,0},{1,5},{5,1},{2,6},{6,2},{3,7},{7,3},{8,12},{12,8},{9,1... | collective-permute-start | bytes 3145736 | tf_op jit(solution)/shard_map/ppermute | solution.py:323
  172.8 1.0 copy-start.14
  184.4 23.6 %all-to-all-start.2 = ((bf16[4,3,128,512]{3,2,1,0:T(8,128)(2,1)}), bf16[4,3,128,512]{3,2,1,0:T(8,128)(2,1)S(1)}, u32[]{:S(2)}, u32[]{:S(2)}) async-start(bf16[4,3,128,512]{3,2,1,0:T(8,128)(2,1)} %get-tuple-element.45), calls=%async_computation.2 | async-start | bytes 3145728 | tf_op jit(solution)/shard_map/all_to_all | solution.py:641
  188.0 10.5 %copy-start.13 = (f32[32,128]{1,0:T(8,128)S(1)}, f32[32,128]{1,0:T(8,128)}, u32[]{:S(2)}) copy-start(f32[32,128]{1,0:T(8,128)} %get-tuple-element.52) | copy-start | bytes 49156
  188.0 11.3 %copy-start.12 = (f32[3,8,512]{2,1,0:T(8,128)S(1)}, f32[3,8,512]{2,1,0:T(8,128)}, u32[]{:S(2)}) copy-start(f32[3,8,512]{2,1,0:T(8,128)} %get-tuple-element.50) | copy-start | bytes 147460
  208.0 39.8 %copy-start.2 = (bf16[4,3,128,512]{3,2,1,0:T(8,128)(2,1)}, bf16[4,3,128,512]{3,2,1,0:T(8,128)(2,1)S(1)}, u32[]{:S(2)}) copy-start(bf16[4,3,128,512]{3,2,1,0:T(8,128)(2,1)S(1)} %all-to-all-done.2.refs_1_) | copy-start | bytes 4718596
  208.0 39.8 %all-to-all-start.1 = ((bf16[4,3,128,512]{3,2,1,0:T(8,128)(2,1)}), bf16[4,3,128,512]{3,2,1,0:T(8,128)(2,1)S(1)}, u32[]{:S(2)}, u32[]{:S(2)}) async-start(bf16[4,3,128,512]{3,2,1,0:T(8,128)(2,1)} %get-tuple-element.44), calls=%async_computation.1 | async-start | bytes 3145728 | tf_op jit(solution)/shard_map/all_to_all | solution.py:641
  211.6 5.9 %collective-permute-start.9 = (f32[32,1024]{1,0:T(8,128)S(1)}, f32[32,1024]{1,0:T(8,128)S(1)}, u32[]{:S(2)}, u32[]{:S(2)}) collective-permute-start(f32[32,1024]{1,0:T(8,128)S(1)} %pad_maximum_fusion), channel_id=1, source_target_pairs={{0,4},{4,0},{1,5},{5,1},{2,6},{6,2},{3,7},{7,3},{8,12},{12,8},{9,1... | collective-permute-start | bytes 393224 | tf_op jit(solution)/shard_map/ppermute | solution.py:327
  217.6 13.7 %collective-permute-start.10 = (f32[32,1024]{1,0:T(8,128)S(1)}, f32[32,1024]{1,0:T(8,128)S(1)}, u32[]{:S(2)}, u32[]{:S(2)}) collective-permute-start(f32[32,1024]{1,0:T(8,128)S(1)} %fusion), channel_id=1, source_target_pairs={{0,8},{8,0},{16,24},{24,16},{1,9},{9,1},{17,25},{25,17},{2,10},{10... | collective-permute-start | bytes 393224 | tf_op jit(solution)/shard_map/ppermute | solution.py:327
  231.3 15.3 %collective-permute-start.11 = (f32[32,1024]{1,0:T(8,128)S(1)}, f32[32,1024]{1,0:T(8,128)S(1)}, u32[]{:S(2)}, u32[]{:S(2)}) collective-permute-start(f32[32,1024]{1,0:T(8,128)S(1)} %add.20), channel_id=1, source_target_pairs={{0,16},{8,24},{16,0},{24,8},{1,17},{9,25},{17,1},{25,9},{2,18},{10... | collective-permute-start | bytes 393224 | tf_op jit(solution)/shard_map/ppermute | solution.py:327
  247.2 8.8 %copy-start.11 = (f32[3,8,1024]{2,1,0:T(8,128)}, f32[3,8,1024]{2,1,0:T(8,128)S(1)}, u32[]{:S(2)}) copy-start(f32[3,8,1024]{2,1,0:T(8,128)S(1)} %slice_bitcast_fusion) | copy-start | bytes 294916
  247.9 1.1 copy-start.3
Sparse Core Ops, SparseCore 0:
  9.6 83.4 all-gather.1
  162.1 84.5 reduce-scatter.1
